TPU v7x, 32 devices: a whole 2x2x4 slice. The times are simulated.
32 devices in a mesh: tm: 4 (over z), space: 8 (over y, x, core).
Axes of the slice: x: 2, y: 2, z: 4, core: 2. Of those that a mesh axis runs over, the one named last changes fastest.
Arguments:
- height_residual: float32 [32, 128, 2048], P('tm', 'space'), may hold values from -6 to 6
- east_residual: float32 [32, 128, 2048], P('tm', 'space'), may hold values from -6 to 6
- north_residual: float32 [32, 128, 2048], P('tm', 'space'), may hold values from -6 to 6
Outputs:
- height_update: float32 [32, 128, 2048], P('tm', 'space')
- east_update: float32 [32, 128, 2048], P('tm', 'space')
- north_update: float32 [32, 128, 2048], P('tm', 'space')
All inputs are finite; a program needn't handle non-finite values.
Results may differ from a plain program's by a relative error of at most 0.00019.
Values sent between devices are 32-bit elements; how exact they have to be, the bound alone decides.
No kernel may reach another device: no remote copies, remote signals or barrier semaphores. Data moves between devices by JAX's collectives and lax.ppermute only.
A program may use at most 128 MiB of HBM per device.

v0:
```python
import math

import jax
import jax.numpy as jnp
from jax import lax
from jax.sharding import PartitionSpec as P

alpha_window = 0.1
gravity = 1.0
mean_depth = 0.25
coriolis = 0.3
wave_speed = gravity * mean_depth


def padded(block, sides, width):
    for axis, dim in sides:
        count = lax.axis_size(axis)
        forward = [(i, i + 1) for i in range(count - 1)]
        forward.append((count - 1, 0))
        backward = [(target, source) for source, target in forward]
        low = lax.ppermute(
            lax.slice_in_dim(block, block.shape[dim] - width, None, axis=dim), axis, forward
        )
        high = lax.ppermute(lax.slice_in_dim(block, 0, width, axis=dim), axis, backward)
        block = jnp.concatenate([low, block, high], axis=dim)
    return block


def partner(x, axis, stride):
    return lax.ppermute(x, axis, [(i, i ^ 1 << stride) for i in range(lax.axis_size(axis))])


def complex_product(first, second):
    return (
        first[0] * second[0] - first[1] * second[1],
        first[0] * second[1] + first[1] * second[0],
    )


def frequency_terms(freqs, steps):
    root_rate = alpha_window ** (1.0 / steps)
    angles = freqs * (2.0 * math.pi / steps)
    spectral_shift = (1.0 - root_rate * jnp.cos(angles), root_rate * jnp.sin(angles))
    square = (
        spectral_shift[0] * spectral_shift[0]
        - spectral_shift[1] * spectral_shift[1]
        + coriolis * coriolis,
        2.0 * spectral_shift[0] * spectral_shift[1],
    )
    shift_norm = spectral_shift[0] * spectral_shift[0] + spectral_shift[1] * spectral_shift[1]
    inv_shift = (spectral_shift[0] / shift_norm, -spectral_shift[1] / shift_norm)
    square_over_shift = complex_product(square, inv_shift)
    turn_over_shift = (coriolis * inv_shift[0], coriolis * inv_shift[1])
    diagonal = (square[0] + 4.0 * wave_speed, square[1])
    diag_norm = diagonal[0] * diagonal[0] + diagonal[1] * diagonal[1]
    inv_diagonal = (diagonal[0] / diag_norm, -diagonal[1] / diag_norm)
    square_norm = square[0] * square[0] + square[1] * square[1]
    inv_square = (square[0] / square_norm, -square[1] / square_norm)
    shift_over_square = complex_product(spectral_shift, inv_square)
    turn_over_square = (coriolis * inv_square[0], coriolis * inv_square[1])
    return (square_over_shift, turn_over_shift, inv_diagonal, shift_over_square, turn_over_square)


def east_diff(values):
    return 0.5 * (jnp.roll(values, -1, -1) - jnp.roll(values, 1, -1))


def north_diff(values):
    return 0.5 * (values[..., 2:, :] - values[..., :-2, :])


def trim_rows(values, margin):
    return values[..., margin : values.shape[-2] - margin, :]


def trim_pair(pair, margin):
    return (trim_rows(pair[0], margin), trim_rows(pair[1], margin))


def neighbours(values):
    return (
        values[..., 2:, :]
        + values[..., :-2, :]
        + trim_rows(jnp.roll(values, -1, -1) + jnp.roll(values, 1, -1), 1)
    )


def helmholtz_source(height, east, north, terms):
    divergence = (
        trim_rows(east_diff(east[0]), 1) + north_diff(north[0]),
        trim_rows(east_diff(east[1]), 1) + north_diff(north[1]),
    )
    vorticity = (
        trim_rows(east_diff(north[0]), 1) - north_diff(east[0]),
        trim_rows(east_diff(north[1]), 1) - north_diff(east[1]),
    )
    turned = complex_product(terms[1], vorticity)
    scaled = complex_product(terms[0], height)
    return (
        scaled[0] - mean_depth * (divergence[0] + turned[0]),
        scaled[1] - mean_depth * (divergence[1] + turned[1]),
    )


def jacobi_sweep(height, source, inv_diagonal):
    total = (
        source[0] + wave_speed * neighbours(height[0]),
        source[1] + wave_speed * neighbours(height[1]),
    )
    return complex_product(total, inv_diagonal)


def velocities(height, east, north, terms):
    east_force = (
        east[0] - gravity * east_diff(trim_rows(height[0], 1)),
        east[1] - gravity * east_diff(trim_rows(height[1], 1)),
    )
    north_force = (
        north[0] - gravity * north_diff(height[0]),
        north[1] - gravity * north_diff(height[1]),
    )
    first = complex_product(terms[3], east_force)
    second = complex_product(terms[4], north_force)
    third = complex_product(terms[3], north_force)
    fourth = complex_product(terms[4], east_force)
    return (
        (first[0] + second[0], first[1] + second[1]),
        (third[0] - fourth[0], third[1] - fourth[1]),
    )


def reverse_bits(value, width):
    result = value * 0
    for level in range(width):
        result = result + (value >> level & 1) * 2 ** (width - 1 - level)
    return result


def matrix_apply(cosines, sines, pair):
    first = jnp.einsum("ak,ckrx->carx", cosines, pair[0], precision=lax.Precision.HIGHEST)
    second = jnp.einsum("ak,ckrx->carx", sines, pair[1], precision=lax.Precision.HIGHEST)
    third = jnp.einsum("ak,ckrx->carx", sines, pair[0], precision=lax.Precision.HIGHEST)
    fourth = jnp.einsum("ak,ckrx->carx", cosines, pair[1], precision=lax.Precision.HIGHEST)
    return (first - second, third + fourth)


def widen_height(height):
    extended = padded(jnp.stack([height[0], height[1]], 0), (("space", 2),), 1)
    return (extended[0], extended[1])


def body(height_residual, east_residual, north_residual):
    steps_local = height_residual.shape[0]
    parts = lax.axis_size("tm")
    levels = parts.bit_length() - 1
    device = lax.axis_index("tm")
    steps = steps_local * parts
    log_rate = math.log(alpha_window) / steps
    local_ids = jnp.arange(steps_local, dtype=jnp.int32)
    step_ids = (device * steps_local + local_ids).astype(jnp.float32)
    weights = jnp.exp(step_ids * log_rate)[:, None, None]
    stacked = jnp.stack(
        [height_residual * weights, east_residual * weights, north_residual * weights], 0
    )
    unweights = jnp.exp(-step_ids * log_rate)[:, None, None]
    reversed_id = reverse_bits(device, levels)
    partner_data = partner(stacked, "tm", levels - 1)
    upper = device >> levels - 1 & 1 == 1
    angles = (device % (parts // 2)).astype(jnp.float32) * (-2.0 * math.pi / parts)
    difference = partner_data - stacked
    real_part = jnp.where(upper, difference * jnp.cos(angles), stacked + partner_data)
    imag_part = jnp.where(upper, difference * jnp.sin(angles), jnp.zeros_like(stacked))
    for level in range(levels - 2, -1, -1):
        span_half = 2**level
        exchanged = partner(jnp.concatenate([real_part, imag_part], 0), "tm", level)
        other = (exchanged[:3], exchanged[3:])
        upper = device >> level & 1 == 1
        angles = (device % span_half).astype(jnp.float32) * (-2.0 * math.pi / (2 * span_half))
        turned = complex_product(
            (other[0] - real_part, other[1] - imag_part), (jnp.cos(angles), jnp.sin(angles))
        )
        real_part, imag_part = (
            jnp.where(upper, turned[0], real_part + other[0]),
            jnp.where(upper, turned[1], imag_part + other[1]),
        )
    angles = (local_ids * reversed_id).astype(jnp.float32) * (-2.0 * math.pi / steps)
    spectrum = complex_product(
        (real_part, imag_part), (jnp.cos(angles)[:, None, None], jnp.sin(angles)[:, None, None])
    )
    angles = (local_ids[:, None] * local_ids[None, :]).astype(jnp.float32) * (
        -2.0 * math.pi / steps_local
    )
    spectrum = matrix_apply(jnp.cos(angles), jnp.sin(angles), spectrum)
    freqs = (reversed_id + parts * local_ids).astype(jnp.float32)
    terms = frequency_terms(freqs[:, None, None], steps)
    height_in = (spectrum[0][0], spectrum[1][0])
    momentum = padded(
        jnp.stack([spectrum[0][1], spectrum[1][1], spectrum[0][2], spectrum[1][2]], 0),
        (("space", 2),),
        1,
    )
    east = (momentum[0], momentum[1])
    north = (momentum[2], momentum[3])
    source = helmholtz_source(height_in, east, north, terms)
    height = complex_product(source, terms[2])
    for sweep_count in range(2):
        height = jacobi_sweep(widen_height(height), source, terms[2])
    east_out, north_out = velocities(
        widen_height(height), trim_pair(east, 1), trim_pair(north, 1), terms
    )
    real_part = jnp.stack([height[0], east_out[0], north_out[0]], 0)
    imag_part = jnp.stack([height[1], east_out[1], north_out[1]], 0)
    angles = (local_ids[:, None] * local_ids[None, :]).astype(jnp.float32) * (
        2.0 * math.pi / steps_local
    )
    result = matrix_apply(jnp.cos(angles), jnp.sin(angles), (real_part, imag_part))
    angles = (local_ids * reversed_id).astype(jnp.float32) * (2.0 * math.pi / steps)
    result = complex_product(
        result, (jnp.cos(angles)[:, None, None], jnp.sin(angles)[:, None, None])
    )
    real_part, imag_part = result
    for level in range(levels):
        span_half = 2**level
        exchanged = partner(jnp.concatenate([real_part, imag_part], 0), "tm", level)
        other = (exchanged[:3], exchanged[3:])
        upper = device >> level & 1 == 1
        angles = (device % span_half).astype(jnp.float32) * (2.0 * math.pi / (2 * span_half))
        twiddle = (jnp.cos(angles), jnp.sin(angles))
        turned_mine = complex_product((real_part, imag_part), twiddle)
        turned_other = complex_product(other, twiddle)
        real_part, imag_part = (
            jnp.where(upper, other[0] - turned_mine[0], real_part + turned_other[0]),
            jnp.where(upper, other[1] - turned_mine[1], imag_part + turned_other[1]),
        )
    final = real_part / steps * unweights
    return (final[0], final[1], final[2])


def solution(mesh):
    in_specs = (P("tm", "space", None), P("tm", "space", None), P("tm", "space", None))
    out_specs = (P("tm", "space", None), P("tm", "space", None), P("tm", "space", None))
    return jax.shard_map(body, mesh=mesh, in_specs=in_specs, out_specs=out_specs, check_vma=False)
```

profile of v0, /device:TPU:0, one launch (start us, length us, event | category | flops | bytes accessed | tf_op | source)
XLA Modules:
  0.0 811.0 jit_solution(2395600445150511835)
XLA Ops:
  0.6 3.7 fusion.52
  6.0 4.0 collective-permute-start
  10.2 135.5 %collective-permute-done = f32[3,8,16,2048]{3,1,2,0:T(8,128)} collective-permute-done((f32[3,8,16,2048]{3,1,2,0:T(8,128)S(1)}, f32[3,8,16,2048]{3,1,2,0:T(8,128)}, u32[]{:S(2)}, u32[]{:S(2)}) %collective-permute-start) | collective-permute-done | bytes 3145760 | tf_op jit(solution)/shard_map/ppermute | solution.py:30
  145.7 3.7 add_select_fusion.4
  149.3 3.4 pad_maximum_fusion
  153.5 136.4 %collective-permute-done.1 = f32[6,8,16,2048]{3,1,2,0:T(8,128)} collective-permute-done((f32[6,8,16,2048]{3,1,2,0:T(8,128)}, f32[6,8,16,2048]{3,1,2,0:T(8,128)}, u32[]{:S(2)}, u32[]{:S(2)}) %collective-permute-start.1) | collective-permute-done | bytes 6291488 | tf_op jit(solution)/shard_map/ppermute | solution.py:30
  289.9 5.3 add_select_fusion.3
  295.1 4.0 fusion.61
  299.1 4.0 fusion.57
  303.1 17.0 %subtract_bitcast_fusion.1 = f32[3,8,16,2048]{3,1,2,0:T(8,128)S(1)} fusion(f32[3,16,2048,8]{2,3,1,0:T(8,128)S(1)} %fusion.61, f32[3,8,16,2048]{3,1,2,0:T(8,128)S(1)} %get-tuple-element.23, f32[3,8,16,2048]{3,1,2,0:T(8,128)S(1)} %get-tuple-element.22, f32[8]{0:T(128)S(1)} %get-tuple-element.103, f32[8]{0:T(128)S(1)} %get-tuple-element.104), kind=kOutput, calls=%fused_computation.17 | convolution fusion | flops 78643392 | bytes 12582976 | tf_op jit(solution)/shard_map/ak,ckrx->carx/dot_general | solution.py:140
  320.4 4.1 add_bitcast_fusion.1
  324.7 2.6 collective-permute-start.3
  327.5 5.0 collective-permute-done.2
  335.2 3.2 subtract_bitcast_fusion.6
  341.4 3.0 collective-permute-done.4
  350.0 3.6 collective-permute-done.6
  357.1 2.0 collective-permute-start.9
  359.3 3.8 collective-permute-done.8
  364.4 1.7 add_bitcast_fusion.2
  366.9 3.6 fusion.5
  370.5 3.6 fusion.4
  374.2 3.7 convolution_add_fusion
  377.9 4.6 add_bitcast_fusion
  384.3 137.1 %collective-permute-done.10 = f32[6,8,16,2048]{3,1,2,0:T(8,128)S(1)} collective-permute-done((f32[6,8,16,2048]{3,1,2,0:T(8,128)S(1)}, f32[6,8,16,2048]{3,1,2,0:T(8,128)S(1)}, u32[]{:S(2)}, u32[]{:S(2)}) %collective-permute-start.10) | collective-permute-done | bytes 6291488 | tf_op jit(solution)/shard_map/ppermute | solution.py:30
  521.4 2.0 add_select_fusion
  523.4 3.4 pad_maximum_fusion.2
  527.0 2.1 collective-permute-start.11
  529.2 271.4 %collective-permute-done.11 = f32[6,8,16,2048]{3,1,2,0:T(8,128)} collective-permute-done((f32[6,8,16,2048]{3,1,2,0:T(8,128)}, f32[6,8,16,2048]{3,1,2,0:T(8,128)}, u32[]{:S(2)}, u32[]{:S(2)}) %collective-permute-start.11) | collective-permute-done | bytes 6291488 | tf_op jit(solution)/shard_map/ppermute | solution.py:30
  800.6 5.2 fusion.3
  806.1 1.6 copy.10
  807.7 1.6 copy.11
  809.2 1.6 copy.9
  (74 shorter events, 22.0 us)
Async XLA Ops:
  4.3 1.0 copy-start.2
  4.3 1.3 copy-start.3
  4.4 1.6 copy-start.4
  6.0 139.7 %collective-permute-start = (f32[3,8,16,2048]{3,1,2,0:T(8,128)S(1)}, f32[3,8,16,2048]{3,1,2,0:T(8,128)}, u32[]{:S(2)}, u32[]{:S(2)}) collective-permute-start(f32[3,8,16,2048]{3,1,2,0:T(8,128)S(1)} %pad_maximum_fusion.4), channel_id=1, source_target_pairs={{0,16},{8,24},{16,0},{24,8},{1,17},{9,25},{17,1},{25,9},{2,18},{10... | collective-permute-start | bytes 9437192 | tf_op jit(solution)/shard_map/ppermute | solution.py:30
  149.3 3.5 copy-start
  152.9 137.0 %collective-permute-start.1 = (f32[6,8,16,2048]{3,1,2,0:T(8,128)}, f32[6,8,16,2048]{3,1,2,0:T(8,128)}, u32[]{:S(2)}, u32[]{:S(2)}) collective-permute-start(f32[6,8,16,2048]{3,1,2,0:T(8,128)} %pad_maximum_fusion), channel_id=1, source_target_pairs={{0,8},{8,0},{16,24},{24,16},{1,9},{9,1},{17,25},{25,17},{2,10},{10... | collective-permute-start | bytes 18874376 | tf_op jit(solution)/shard_map/ppermute | solution.py:30
  324.7 7.9 collective-permute-start.2
  324.7 7.8 collective-permute-start.3
  338.7 5.7 collective-permute-start.4
  340.0 4.4 collective-permute-start.5
  347.3 6.3 collective-permute-start.6
  348.8 4.8 collective-permute-start.7
  356.5 6.6 collective-permute-start.8
  357.1 6.0 collective-permute-start.9
  383.2 138.1 %collective-permute-start.10 = (f32[6,8,16,2048]{3,1,2,0:T(8,128)S(1)}, f32[6,8,16,2048]{3,1,2,0:T(8,128)S(1)}, u32[]{:S(2)}, u32[]{:S(2)}) collective-permute-start(f32[6,8,16,2048]{3,1,2,0:T(8,128)S(1)} %pad_maximum_fusion.1), channel_id=1, source_target_pairs={{0,8},{8,0},{16,24},{24,16},{1,9},{9,1},{17,25},{25,17},{2,10},{10... | collective-permute-start | bytes 18874376 | tf_op jit(solution)/shard_map/ppermute | solution.py:30
  523.4 3.5 copy-start.1
  527.0 273.7 %collective-permute-start.11 = (f32[6,8,16,2048]{3,1,2,0:T(8,128)}, f32[6,8,16,2048]{3,1,2,0:T(8,128)}, u32[]{:S(2)}, u32[]{:S(2)}) collective-permute-start(f32[6,8,16,2048]{3,1,2,0:T(8,128)} %pad_maximum_fusion.2), channel_id=1, source_target_pairs={{0,16},{8,24},{16,0},{24,8},{1,17},{9,25},{17,1},{25,9},{2,18},{10... | collective-permute-start | bytes 18874376 | tf_op jit(solution)/shard_map/ppermute | solution.py:30
where the time goes:
time: 813 us; the launch traced here: 811 us
  waiting for transfers between devices  696 us (86%)
  matrix products  44.5 us (5%)
  other arithmetic  37.8 us (5%)
  starting transfers between devices  18.6 us (2%)
  local copies, waits for them, and re-layouts  12.8 us (2%)
    ppermute x4, waiting for transfers between devices, partner(): lax.ppermute(x, axis, [(i, i ^ 1 << stride) for i in range(lax.axis_size(...  680 us
    dot_general x2, matrix products, matrix_apply(): jnp.einsum('ak,ckrx->carx', cosines, pair[0], precision=lax.Precision.HIG...  20.6 us
  transfers between devices with their start and end apart: 12, of which 8 were waited for; matrix products, arithmetic and copies ran while one was open for 0% of the time, Pallas kernels for 0%

commit v1 on v0

v1 whole, which is shorter than its diff:
```python
import functools
import math

import jax
import jax.numpy as jnp
import numpy as np
from jax import lax
from jax.experimental import pallas as pl
from jax.experimental.pallas import tpu as pltpu
from jax.sharding import PartitionSpec as P

alpha_window = 0.1
gravity = 1.0
mean_depth = 0.25
coriolis = 0.3
wave_speed = gravity * mean_depth
diagonal = 1.0 + coriolis * coriolis + 4.0 * wave_speed
turn_norm = 1.0 / (1.0 + coriolis * coriolis)
LANES = 128
MIB = 1 << 20

WIDTH = (1, 3, 3, 5, 5, 7, 7)
ENTRIES = [(i, j) for i in range(7) for j in range(WIDTH[i])]


def step_matrix():
    m = np.zeros((7, 7))
    m[0, 0] = 1.0
    source = np.zeros(7)
    source[0] = coriolis
    for k in range(3):
        u, r = 1 + 2 * k, 2 + 2 * k
        new = source.copy()
        new[u] += 1.0
        new = new / diagonal
        m[r] = new
        m[u] = 2.0 * new
        m[u, r] -= 1.0
        source = wave_speed * new
    return m


def tables(parts, steps_local):
    one = step_matrix()
    turn = 1.0 / (1.0 + 1j * coriolis)
    block = np.linalg.matrix_power(one, steps_local)
    spin = turn**steps_local
    power = lambda k: np.linalg.matrix_power(block, k)
    closure = np.linalg.inv(np.eye(7) - alpha_window * power(parts))
    closure_spin = 1.0 / (1.0 - alpha_window * spin**parts)
    zero, eye = np.zeros((7, 7)), np.eye(7)
    fields, turns = [], []
    for b in range(parts):
        row, spins = [], []
        row.append(alpha_window * closure @ power(parts - 1))
        spins.append(alpha_window * closure_spin * spin ** (parts - 1))
        for hop in range(1, parts):
            if hop == b:
                row.append(closure)
                spins.append(closure_spin)
            elif hop == parts - 1 - b:
                row.append(alpha_window * closure @ power(b))
                spins.append(alpha_window * closure_spin * spin**b)
            else:
                row.append(zero)
                spins.append(0.0)
            following = hop + 1
            if b == following - 1:
                row += [block, eye]
                spins += [spin, 1.0]
            elif b == parts - following:
                row += [eye, power(parts - 1 - b)]
                spins += [1.0, spin ** (parts - 1 - b)]
            else:
                row += [zero, zero]
                spins += [0.0, 0.0]
        fields.append(np.concatenate([[m[i, j] for i, j in ENTRIES] for m in row]))
        turns.append(np.concatenate([[np.real(s), np.imag(s)] for s in spins]))
    return np.concatenate([np.array(fields), np.array(turns)], axis=1).astype(np.float32)


def start_rows():
    one = step_matrix()
    inverse = np.linalg.inv((1.0 + 1j * coriolis) * one - np.eye(7))
    return [one[2 + 2 * k] @ inverse for k in range(3)]


def low_half(shape):
    return lax.broadcasted_iota(jnp.int32, shape, len(shape) - 2) < 4


def wide(load, start, width, total):
    left = pl.multiple_of(lax.rem(start + (total - LANES), total), LANES)
    right = pl.multiple_of(lax.rem(start + width, total), LANES)
    return jnp.concatenate(
        [load(pl.ds(left, LANES)), load(pl.ds(start, width)), load(pl.ds(right, LANES))], axis=-1
    )


def core(x):
    return x[:, LANES : x.shape[1] - LANES]


def next_column(x):
    return core(pltpu.roll(x, x.shape[1] - 1, 1))


def previous_column(x):
    return core(pltpu.roll(x, 1, 1))


def next_row(x):
    return pltpu.roll(x, x.shape[0] - 1, 0)


def previous_row(x):
    return pltpu.roll(x, 1, 0)


def dx(x):
    return 0.5 * (next_column(x) - previous_column(x))


def dy(x):
    return 0.5 * (next_row(x) - previous_row(x))


def neighbours(x):
    middle = core(x)
    return (next_row(middle) + previous_row(middle)) + (next_column(x) + previous_column(x))


def turn_kernel(e_ref, n_ref, out_ref, *, width):
    steps, _, total = e_ref.shape

    def block(i, carry):
        cols = pl.ds(pl.multiple_of(i * width, width), width)
        re, im = e_ref[0, :, cols], n_ref[0, :, cols]
        re, im = turn_norm * (re + coriolis * im), turn_norm * (im - coriolis * re)
        for step in range(1, steps):
            re, im = re + e_ref[step, :, cols], im + n_ref[step, :, cols]
            re, im = turn_norm * (re + coriolis * im), turn_norm * (im - coriolis * re)
        out_ref[0, :, cols] = re
        out_ref[1, :, cols] = im
        return carry

    lax.fori_loop(0, total // width, block, 0)


def source_kernel(
    h_ref, e_ref, n_ref, before_ref, after_ref, src_ref, edge_ref, inner_ref, prev_ref, next_ref, *, width
):
    steps, rows, total = h_ref.shape

    def block(i, carry):
        start = pl.multiple_of(i * width, width)
        cols = pl.ds(start, width)
        row = lax.broadcasted_iota(jnp.int32, (rows, width), 0)
        first, last = row == 0, row == rows - 1
        low = low_half((8, width))

        def slopes(ref, step, at):
            x = wide(lambda c: ref[step, :, c], start, width, total)
            mid = core(x)
            line = pl.ds(at + step, 1)
            up = jnp.where(last, after_ref[line, cols], next_row(mid))
            down = jnp.where(first, before_ref[line, cols], previous_row(mid))
            return dx(x), 0.5 * (up - down)

        p = jnp.zeros((rows, width), jnp.float32)
        state = [p] * 6
        held = None
        h_last = None
        for step in range(steps):
            h = h_ref[step, :, cols]
            e_x, e_y = slopes(e_ref, step, 0)
            n_x, n_y = slopes(n_ref, step, steps)
            p = p + (coriolis * h - mean_depth * (n_x - e_y))
            change = h if h_last is None else h - h_last
            src = (change - mean_depth * (e_x + n_y)) + coriolis * p
            h_last = h
            src_ref[step, :, cols] = src
            top, bottom = src[:8], src[8:]
            if step % 2 == 0:
                held = (top, bottom)
            else:
                prev_ref[step // 2, :, cols] = jnp.where(low, held[0], pltpu.roll(top, 4, 0))
                next_ref[step // 2, :, cols] = jnp.where(low, pltpu.roll(bottom, 4, 0), held[1])
            state = advance(src, state)
        state[0] = state[0] - h_last
        for k, value in enumerate([p] + state):
            top, bottom = value[:8], value[8:]
            edge_ref[k, :, cols] = jnp.where(low, top, bottom)
            inner_ref[k, :, cols] = jnp.where(low, bottom, top)
        return carry

    lax.fori_loop(0, total // width, block, 0)


def advance(source, state):
    out, x = [], source
    for k in range(3):
        u, r = state[2 * k], state[2 * k + 1]
        new = (x + u) * (1.0 / diagonal)
        out += [2.0 * new - r, new]
        x = wave_speed * new
    return out


def apply_matrix(coef_ref, at, fields):
    out, pos = [], at
    for i in range(7):
        total = None
        for j in range(WIDTH[i]):
            term = coef_ref[pos] * fields[j]
            total = term if total is None else total + term
            pos += 1
        out.append(total)
    return out


def apply_turn(coef_ref, at, fields):
    c, s = coef_ref[at], coef_ref[at + 1]
    return [c * fields[0] - s * fields[1], c * fields[1] + s * fields[0]]


def combine_kernel(coef_ref, *refs, hop, parts, apply, base, size, width):
    refs = list(refs)
    got_ref, own_ref = refs[0], refs[1]
    acc_ref = refs[2] if hop > 1 else None
    outs = refs[3:] if hop > 1 else refs[2:]
    count, _, total = own_ref.shape
    at = base + size * (1 + 3 * (hop - 1))

    def block(i, carry):
        cols = pl.ds(pl.multiple_of(i * width, width), width)
        got = [got_ref[k, :, cols] for k in range(count)]
        part = apply(coef_ref, at, got)
        own = None
        if hop == 1 or hop < parts - 1:
            own = [own_ref[k, :, cols] for k in range(count)]
        if hop == 1:
            base_part = apply(coef_ref, base, own)
        else:
            base_part = [acc_ref[k, :, cols] for k in range(count)]
        for k in range(count):
            outs[0][k, :, cols] = base_part[k] + part[k]
        if hop < parts - 1:
            moved = apply(coef_ref, at + size, got)
            added = apply(coef_ref, at + 2 * size, own)
            for k in range(count):
                outs[1][k, :, cols] = moved[k] + added[k]
        return carry

    lax.fori_loop(0, total // width, block, 0)


def pack_kernel(edge_ref, phi_ref, prev_ref, next_ref, *, width):
    total = edge_ref.shape[2]

    def block(i, carry):
        cols = pl.ds(pl.multiple_of(i * width, width), width)
        low = low_half((8, width))
        tops = [edge_ref[k, :, cols] for k in range(7)] + [phi_ref[k, :8, cols] for k in range(2)]
        bottoms = tops[:7] + [phi_ref[k, 8:, cols] for k in range(2)]
        for t in range(5):
            a, b = 2 * t, min(2 * t + 1, 8)
            prev_ref[t, :, cols] = jnp.where(low, tops[a], pltpu.roll(tops[b], 4, 0))
            next_ref[t, :, cols] = jnp.where(low, pltpu.roll(bottoms[b], 4, 0), bottoms[a])
        return carry

    lax.fori_loop(0, total // width, block, 0)


def unpack(from_next, from_prev, odd, low):
    if odd:
        return pltpu.roll(jnp.where(low, from_prev, from_next), 4, 0)
    return jnp.where(low, from_next, from_prev)


def final_kernel(
    edge_ref, inner_ref, phi_ref, s_after_ref, s_before_ref, src_ref, src_after_ref, src_before_ref,
    e_hbm, n_hbm, h_out, e_out, n_out, r1, r2, r3, ring, e_ref, n_ref, u_ref, v_ref, sems, *, width
):
    steps, rows, total = src_ref.shape
    copies_in = [
        pltpu.make_async_copy(e_hbm, e_ref, sems.at[0]),
        pltpu.make_async_copy(n_hbm, n_ref, sems.at[1]),
    ]
    for copy in copies_in:
        copy.start()
    lines = [np.asarray(line) for line in start_rows()]

    def filters(i, carry):
        cols = pl.ds(pl.multiple_of(i * width, width), width)
        low = low_half((8, width))
        fields = []
        for k in range(9):
            halo = unpack(s_after_ref[k // 2, :, cols], s_before_ref[k // 2, :, cols], k % 2 == 1, low)
            if k < 7:
                edge, inner = edge_ref[k, :, cols], inner_ref[k, :, cols]
                fields.append(
                    jnp.concatenate([jnp.where(low, edge, inner), jnp.where(low, inner, edge), halo], 0)
                )
            else:
                ring[k - 7, :, cols] = jnp.concatenate([phi_ref[k - 7, :, cols], halo], 0)
        for planes, line in ((r1, lines[0]), (r2, lines[1]), (r3, lines[2])):
            for part, weights in ((0, np.real(line)), (1, np.imag(line))):
                value = None
                for j in range(7):
                    if weights[j] != 0.0:
                        term = float(weights[j]) * fields[j]
                        value = term if value is None else value + term
                planes[steps + part, :, cols] = value
        turned = coriolis * fields[0]
        state = fields[1:]
        for step in range(steps):
            pair = step // 2
            halo = unpack(src_after_ref[pair, :, cols], src_before_ref[pair, :, cols], step % 2 == 1, low)
            source = jnp.concatenate([src_ref[step, :, cols], halo], 0) + turned
            state = advance(source, state)
            r1[step, :, cols] = state[1]
            r2[step, :, cols] = state[3]
            r3[step, :, cols] = state[5]
        return carry

    lax.fori_loop(0, total // width, filters, 0)

    def over_blocks(body):
        def at(i, carry):
            start = pl.multiple_of(i * width, width)
            body(start, pl.ds(start, width))
            return carry

        lax.fori_loop(0, total // width, at, 0)

    def spin_terms(start, cols):
        re = wide(lambda c: ring[0, :, c], start, width, total)
        im = wide(lambda c: ring[1, :, c], start, width, total)
        chi = (dx(re) + dy(core(im)), dx(im) - dy(core(re)))
        share = mean_depth / (4.0 * wave_speed)
        for part in range(2):
            r1[steps + part, :, cols] = r1[steps + part, :, cols] - share * chi[part]
            r2[steps + part, :, cols] = r2[steps + part, :, cols] - (share / 4.0) * chi[part]
            r3[steps + part, :, cols] = r3[steps + part, :, cols] - (share / 16.0) * chi[part]

    over_blocks(spin_terms)

    def horner(low_ref, high_ref):
        def body(start, cols):
            def plane(k, carry):
                x = wide(lambda c: high_ref[k, :, c], start, width, total)
                low_ref[k, :, cols] = low_ref[k, :, cols] + neighbours(x)
                return carry

            lax.fori_loop(0, steps + 2, plane, 0)

        over_blocks(body)

    horner(r2, r3)
    horner(r1, r2)
    height_copy = pltpu.make_async_copy(r1.at[pl.ds(0, steps), pl.ds(0, rows)], h_out, sems.at[2])
    height_copy.start()
    for copy in copies_in:
        copy.wait()

    def velocity(start, cols):
        def slopes(k):
            x = wide(lambda c: r1[k, :, c], start, width, total)
            return dx(x)[:rows], dy(core(x))[:rows]

        re_x, re_y = slopes(steps)
        im_x, im_y = slopes(steps + 1)
        u = ring[0, :rows, cols] - gravity * (re_x - im_y)
        v = ring[1, :rows, cols] - gravity * (im_x + re_y)
        for step in range(steps):
            eta_x, eta_y = slopes(step)
            re = u + (e_ref[step, :, cols] - gravity * eta_x)
            im = v + (n_ref[step, :, cols] - gravity * eta_y)
            u, v = turn_norm * (re + coriolis * im), turn_norm * (im - coriolis * re)
            u_ref[step, :, cols] = u
            v_ref[step, :, cols] = v

    over_blocks(velocity)
    copies_out = [
        pltpu.make_async_copy(u_ref, e_out, sems.at[3]),
        pltpu.make_async_copy(v_ref, n_out, sems.at[4]),
    ]
    for copy in copies_out:
        copy.start()
    for copy in copies_out:
        copy.wait()
    height_copy.wait()


VMEM = pl.BlockSpec(memory_space=pltpu.VMEM)
SMEM = pl.BlockSpec(memory_space=pltpu.SMEM)
ANY = pl.BlockSpec(memory_space=pl.ANY)


def f32(*shape):
    return jax.ShapeDtypeStruct(shape, jnp.float32)


def call(kernel, args, outs, in_specs=None, name=None, limit=24, scratch=(), out_specs=None):
    return pl.pallas_call(
        kernel,
        out_shape=outs,
        in_specs=in_specs or [VMEM] * len(args),
        out_specs=out_specs or [VMEM] * len(outs),
        scratch_shapes=scratch,
        compiler_params=pltpu.CompilerParams(vmem_limit_bytes=limit * MIB),
        name=name,
    )(*args)


def shifts(axis):
    count = lax.axis_size(axis)
    forward = [(i, (i + 1) % count) for i in range(count)]
    return forward, [(t, s) for s, t in forward]


def body(h, e, n):
    steps, rows, total = h.shape
    parts = lax.axis_size("tm")
    width = 512 if total % 512 == 0 else LANES
    coef = jnp.asarray(tables(parts, steps))[lax.axis_index("tm")]
    turn_base = len(ENTRIES) * (1 + 3 * (parts - 1))
    forward, backward = shifts("space")

    before = lax.ppermute(jnp.concatenate([e[:, rows - 1], n[:, rows - 1]], 0), "space", forward)
    after = lax.ppermute(jnp.concatenate([e[:, 0], n[:, 0]], 0), "space", backward)

    def hop(x, k):
        return lax.ppermute(x, "tm", [(k - 1, k), (parts - k, parts - 1 - k)])

    def combine(k, got, own, acc, kind):
        apply, base, size = {
            "fields": (apply_matrix, 0, len(ENTRIES)),
            "turn": (apply_turn, turn_base, 2),
        }[kind]
        args = [coef, got, own] + ([acc] if k > 1 else [])
        outs = [f32(*own.shape)] * (2 if k < parts - 1 else 1)
        kernel = functools.partial(
            combine_kernel, hop=k, parts=parts, apply=apply, base=base, size=size,
            width=min(width, own.shape[2]),
        )
        return call(kernel, args, outs, [SMEM] + [VMEM] * (len(args) - 1), f"combine_{kind}_{k}")

    phi = call(functools.partial(turn_kernel, width=width), [e, n], [f32(2, rows, total)], name="turn")[0]
    tile = f32(7, 8, total)
    src, edge, inner, src_prev, src_next = call(
        functools.partial(source_kernel, width=width),
        [h, e, n, before, after],
        [f32(steps, rows, total), tile, tile, f32(steps // 2, 8, total), f32(steps // 2, 8, total)],
        name="source",
    )
    src_after = lax.ppermute(src_prev, "space", backward)
    src_before = lax.ppermute(src_next, "space", forward)

    chunks = [("turn", phi), ("fields", edge), ("fields", inner)]
    message = [c[1] for c in chunks]
    acc = [None] * len(chunks)
    for k in range(1, parts):
        for j, (kind, own) in enumerate(chunks):
            out = combine(k, hop(message[j], k), own, acc[j], kind)
            acc[j] = out[0]
            message[j] = out[1] if k < parts - 1 else None
    phi_in, edge_in, inner_in = acc

    to_prev, to_next = call(
        functools.partial(pack_kernel, width=width), [edge_in, phi_in], [f32(5, 8, total)] * 2, name="pack"
    )
    s_after = lax.ppermute(to_prev, "space", backward)
    s_before = lax.ppermute(to_next, "space", forward)

    planes = pltpu.VMEM((steps + 2, rows + 8, total), jnp.float32)
    whole = pltpu.VMEM((steps, rows, total), jnp.float32)
    return tuple(
        call(
            functools.partial(final_kernel, width=width),
            [edge_in, inner_in, phi_in, s_after, s_before, src, src_after, src_before, e, n],
            [f32(steps, rows, total)] * 3,
            [VMEM] * 8 + [ANY] * 2,
            "final",
            32,
            [planes, planes, planes, pltpu.VMEM((2, rows + 8, total), jnp.float32)]
            + [whole] * 4
            + [pltpu.SemaphoreType.DMA((5,))],
            [ANY] * 3,
        )
    )


def solution(mesh):
    specs = (P("tm", "space", None),) * 3
    return jax.shard_map(body, mesh=mesh, in_specs=specs, out_specs=specs, check_vma=False)
```

time: 813 us -> 106 us (0.13)
  waiting for transfers between devices: 696 us -> 46.5 us
  matrix products: 44.5 us -> 0 us
  other arithmetic: 37.8 us -> 0.02 us
  Pallas kernels: 0 us -> 24.2 us
    ppermute x12 -> x15, waiting for transfers between devices: 696 us -> 46.5 us  [the longest x9 36.3 us: hop(): return lax.ppermute(x, 'tm', [(k - 1, k), (parts - k, parts - 1 - k)])]
    dot_general x8 -> x0, matrix products: 44.5 us -> none  [the longest x2 20.6 us: matrix_apply(): jnp.einsum('ak,ckrx->carx', cosines, pair[0], precision=lax.Precision.HIG...]
    pallas_call x0 -> x13, Pallas kernels: none -> 24.2 us  [call(): pl.pallas_call(kernel, out_shape=outs, in_specs=in_specs or [VMEM] * len(...]
    another operation x10 -> x0, other arithmetic: 12.6 us -> none  [the longest x5 5 us: widen_height(): extended = padded(jnp.stack([height[0], height[1]], 0), (('space', 2),), 1)]
    select_n x3 -> x0, other arithmetic: 11 us -> none  [the longest x1 5.25 us: body(): jnp.where(upper, turned[0], real_part + other[0])]
    concatenate x7 -> x2, other arithmetic: 8.5 us -> 0.02 us  [the longest x1 0.01 us: body(): jnp.concatenate([e[:, rows - 1], n[:, rows - 1]], 0)]
    ppermute x12 -> x15, starting transfers between devices: 18.6 us -> 25.2 us  [the longest x9 19.3 us: hop(): return lax.ppermute(x, 'tm', [(k - 1, k), (parts - k, parts - 1 - k)])]
  transfers between devices with their start and end apart: 12 -> 15, of which waited for: 8 -> 8; matrix products, arithmetic and copies ran while one was open for 0% -> 1% of each run, Pallas kernels for 0% -> 8%
where the time goes in v1:
time: 106 us; the launch traced here: 105 us
  waiting for transfers between devices  46.5 us (44%)
  starting transfers between devices  25.2 us (24%)
  Pallas kernels  24.2 us (23%)
  local copies, waits for them, and re-layouts  8.6 us (8%)
    ppermute x9, waiting for transfers between devices, hop(): return lax.ppermute(x, 'tm', [(k - 1, k), (parts - k, parts - 1 - k)])  36.3 us
    pallas_call x13, Pallas kernels, call(): pl.pallas_call(kernel, out_shape=outs, in_specs=in_specs or [VMEM] * len(...  24.2 us
    ppermute x9, starting transfers between devices, hop(): return lax.ppermute(x, 'tm', [(k - 1, k), (parts - k, parts - 1 - k)])  19.3 us
    ppermute x1, waiting for transfers between devices, body(): src_after = lax.ppermute(src_prev, 'space', backward)  5.41 us
    unnamed x20, local copies, waits for them, and re-layouts  5.12 us
    ppermute x1, starting transfers between devices, body(): lax.ppermute(jnp.concatenate([e[:, 0], n[:, 0]], 0), 'space', backward)  2.95 us
    ppermute x1, waiting for transfers between devices, body(): lax.ppermute(jnp.concatenate([e[:, rows - 1], n[:, rows - 1]], 0), 'space...  2.52 us
  transfers between devices with their start and end apart: 15, of which 8 were waited for; matrix products, arithmetic and copies ran while one was open for 1% of the time, Pallas kernels for 8%

profile of v1, /device:TPU:0, one launch (start us, length us, event | category | flops | bytes accessed | tf_op | source)
XLA Modules:
  0.0 105.4 jit_solution(457252812807017330)
XLA Ops:
  0.6 1.4 %fusion = (f32[8,1,2048]{2,1,0:T(1,128)S(1)}, f32[8,1,2048]{2,1,0:T(1,128)S(1)}) fusion(f32[8,16,2048]{2,1,0:T(8,128)} %e_hbm.1), kind=kLoop, calls=%fused_computation.7 | loop fusion | bytes 262144 | tf_op jit(solution)/shard_map/slice | solution.py:432
  2.0 1.3 %fusion.1 = (f32[8,1,2048]{2,1,0:T(1,128)S(1)}, f32[8,1,2048]{2,1,0:T(1,128)S(1)}) fusion(f32[8,16,2048]{2,1,0:T(8,128)} %n_hbm.1), kind=kLoop, calls=%fused_computation.8 | loop fusion | bytes 262144 | tf_op jit(solution)/shard_map/slice | solution.py:432
  4.0 3.0 %collective-permute-start.1 = (f32[16,2048]{1,0:T(8,128)S(1)}, f32[16,2048]{1,0:T(8,128)S(1)}, u32[]{:S(2)}, u32[]{:S(2)}) collective-permute-start(f32[16,2048]{1,0:T(8,128)S(1)} %pad_maximum_fusion.1), channel_id=1, source_target_pairs={{1,0},{2,1},{3,2},{4,3},{5,4},{6,5},{7,6},{0,7},{9,8},{10,9},{11,1... | collective-permute-start | bytes 393224 | tf_op jit(solution)/shard_map/ppermute | solution.py:432
  6.9 2.5 %collective-permute-done.before_ref = f32[16,2048]{1,0:T(8,128)S(1)} collective-permute-done((f32[16,2048]{1,0:T(8,128)S(1)}, f32[16,2048]{1,0:T(8,128)S(1)}, u32[]{:S(2)}, u32[]{:S(2)}) %collective-permute-start) | collective-permute-done | bytes 131104 | tf_op jit(solution)/shard_map/ppermute | solution.py:431
  9.7 1.2 %copy-done.1 = f32[8,16,2048]{2,1,0:T(8,128)S(1)} copy-done((f32[8,16,2048]{2,1,0:T(8,128)S(1)}, f32[8,16,2048]{2,1,0:T(8,128)}, u32[]{:S(2)}) %copy-start.1) | copy-done | bytes 1048600
  10.9 1.2 %copy-done.3 = f32[8,16,2048]{2,1,0:T(8,128)S(1)} copy-done((f32[8,16,2048]{2,1,0:T(8,128)S(1)}, f32[8,16,2048]{2,1,0:T(8,128)}, u32[]{:S(2)}) %copy-start.3) | copy-done | bytes 1048600
  12.2 2.3 %source.1 = (f32[8,16,2048]{2,1,0:T(8,128)S(1)}, f32[7,8,2048]{2,1,0:T(8,128)S(1)}, f32[7,8,2048]{2,1,0:T(8,128)S(1)}, f32[4,8,2048]{2,1,0:T(8,128)S(1)}, f32[4,8,2048]{2,1,0:T(8,128)S(1)}) custom-call(f32[8,16,2048]{2,1,0:T(8,128)S(1)} %copy-done.3, f32[8,16,2048]{2,1,0:T(8,128)S(1)} %copy-done, f32[8,16,2048]{2,1,0:T(8,128)S(1)} %copy-done.1, ...), custom_call_target="tpu_custom_call" | custom-call | tf_op jit(solution)/shard_map/source/pallas_call | solution.py:406
  14.5 1.0 copy-done.4
  15.4 0.7 copy-done.6
  16.1 0.7 copy-done.8
  16.8 4.7 %collective-permute-start.2 = (f32[7,8,2048]{2,1,0:T(8,128)S(1)}, f32[7,8,2048]{2,1,0:T(8,128)}, u32[]{:S(2)}, u32[]{:S(2)}) collective-permute-start(f32[7,8,2048]{2,1,0:T(8,128)S(1)} %get-tuple-element.22.refs_1_), channel_id=1, source_target_pairs={{0,8},{24,16},{1,9},{25,17},{2,10},{26,18},{3,11},{27,19},{4,12},{... | collective-permute-start | bytes 1376264 | tf_op jit(solution)/shard_map/ppermute | solution.py:435
  21.6 1.3 %collective-permute-start.5 = (f32[7,8,2048]{2,1,0:T(8,128)S(1)}, f32[7,8,2048]{2,1,0:T(8,128)S(1)}, u32[]{:S(2)}, u32[]{:S(2)}) collective-permute-start(f32[7,8,2048]{2,1,0:T(8,128)S(1)} %get-tuple-element.27.refs_1_), channel_id=1, source_target_pairs={{0,8},{24,16},{1,9},{25,17},{2,10},{26,18},{3,11},{27,19},{4,12},{... | collective-permute-start | bytes 1376264 | tf_op jit(solution)/shard_map/ppermute | solution.py:435
  22.9 0.7 dynamic-slice_reduce_fusion.coef_ref
  23.6 7.8 %collective-permute-done.2.refs_0_ = f32[7,8,2048]{2,1,0:T(8,128)} collective-permute-done((f32[7,8,2048]{2,1,0:T(8,128)S(1)}, f32[7,8,2048]{2,1,0:T(8,128)}, u32[]{:S(2)}, u32[]{:S(2)}) %collective-permute-start.2) | collective-permute-done | bytes 458784 | tf_op jit(solution)/shard_map/ppermute | solution.py:435
  31.4 1.6 %combine_fields_1.2 = (f32[7,8,2048]{2,1,0:T(8,128)S(1)}, f32[7,8,2048]{2,1,0:T(8,128)S(1)}) custom-call(f32[330]{0:T(512)S(1)} %dynamic-slice_reduce_fusion.coef_ref, f32[7,8,2048]{2,1,0:T(8,128)} %collective-permute-done.2.refs_0_, f32[7,8,2048]{2,1,0:T(8,128)S(1)} %get-tuple-element.22.refs_1_), custom_call_target="tpu_custom_call" | custom-call | tf_op jit(solution)/shard_map/combine_fields_1/pallas_call | solution.py:406
  34.1 7.3 %collective-permute-start.8 = (f32[2,16,2048]{2,1,0:T(8,128)S(1)}, f32[2,16,2048]{2,1,0:T(8,128)S(1)}, u32[]{:S(2)}, u32[]{:S(2)}) collective-permute-start(f32[2,16,2048]{2,1,0:T(8,128)S(1)} %turn.1.refs_1_), channel_id=1, source_target_pairs={{0,8},{24,16},{1,9},{25,17},{2,10},{26,18},{3,11},{27,19},{4,12},{... | collective-permute-start | bytes 786440 | tf_op jit(solution)/shard_map/ppermute | solution.py:435
  41.4 1.2 %combine_fields_1.3 = (f32[7,8,2048]{2,1,0:T(8,128)S(1)}, f32[7,8,2048]{2,1,0:T(8,128)S(1)}) custom-call(f32[330]{0:T(512)S(1)} %dynamic-slice_reduce_fusion.coef_ref, f32[7,8,2048]{2,1,0:T(8,128)S(1)} %collective-permute-done.5.refs_0_, f32[7,8,2048]{2,1,0:T(8,128)S(1)} %get-tuple-element.27.refs_1_), custom_call_target="tpu_custom_call" | custom-call | tf_op jit(solution)/shard_map/combine_fields_1/pallas_call | solution.py:406
  43.2 4.2 %collective-permute-done.8.refs_0_ = f32[2,16,2048]{2,1,0:T(8,128)S(1)} collective-permute-done((f32[2,16,2048]{2,1,0:T(8,128)S(1)}, f32[2,16,2048]{2,1,0:T(8,128)S(1)}, u32[]{:S(2)}, u32[]{:S(2)}) %collective-permute-start.8) | collective-permute-done | bytes 262176 | tf_op jit(solution)/shard_map/ppermute | solution.py:435
  47.4 0.7 combine_turn_1.1
  48.8 1.0 combine_fields_2.2
  49.8 1.3 %collective-permute-start.4 = (f32[7,8,2048]{2,1,0:T(8,128)S(1)}, f32[7,8,2048]{2,1,0:T(8,128)S(1)}, u32[]{:S(2)}, u32[]{:S(2)}) collective-permute-start(f32[7,8,2048]{2,1,0:T(8,128)S(1)} %get-tuple-element.25), channel_id=1, source_target_pairs={{16,24},{8,0},{17,25},{9,1},{18,26},{10,2},{19,27},{11,3},{20,28},... | collective-permute-start | bytes 1376264 | tf_op jit(solution)/shard_map/ppermute | solution.py:435
  51.8 1.3 %collective-permute-start.10 = (f32[2,16,2048]{2,1,0:T(8,128)S(1)}, f32[2,16,2048]{2,1,0:T(8,128)S(1)}, u32[]{:S(2)}, u32[]{:S(2)}) collective-permute-start(f32[2,16,2048]{2,1,0:T(8,128)S(1)} %get-tuple-element.34), channel_id=1, source_target_pairs={{16,24},{8,0},{17,25},{9,1},{18,26},{10,2},{19,27},{11,3},{20,28},... | collective-permute-start | bytes 786440 | tf_op jit(solution)/shard_map/ppermute | solution.py:435
  53.1 1.0 combine_fields_2.3
  54.2 1.3 %collective-permute-start.7 = (f32[7,8,2048]{2,1,0:T(8,128)S(1)}, f32[7,8,2048]{2,1,0:T(8,128)S(1)}, u32[]{:S(2)}, u32[]{:S(2)}) collective-permute-start(f32[7,8,2048]{2,1,0:T(8,128)S(1)} %get-tuple-element.30), channel_id=1, source_target_pairs={{16,24},{8,0},{17,25},{9,1},{18,26},{10,2},{19,27},{11,3},{20,28},... | collective-permute-start | bytes 1376264 | tf_op jit(solution)/shard_map/ppermute | solution.py:435
  55.5 19.6 %collective-permute-done.10.refs_0_ = f32[2,16,2048]{2,1,0:T(8,128)S(1)} collective-permute-done((f32[2,16,2048]{2,1,0:T(8,128)S(1)}, f32[2,16,2048]{2,1,0:T(8,128)S(1)}, u32[]{:S(2)}, u32[]{:S(2)}) %collective-permute-start.10) | collective-permute-done | bytes 262176 | tf_op jit(solution)/shard_map/ppermute | solution.py:435
  75.7 0.7 combine_fields_3.2.edge_ref
  77.5 1.9 %collective-permute-start.13 = (f32[4,8,2048]{2,1,0:T(8,128)S(1)}, f32[4,8,2048]{2,1,0:T(8,128)S(1)}, u32[]{:S(2)}, u32[]{:S(2)}) collective-permute-start(f32[4,8,2048]{2,1,0:T(8,128)S(1)} %copy-done.9), channel_id=1, source_target_pairs={{1,0},{2,1},{3,2},{4,3},{5,4},{6,5},{7,6},{0,7},{9,8},{10,9},{11,1... | collective-permute-start | bytes 786440 | tf_op jit(solution)/shard_map/ppermute | solution.py:458
  79.4 4.7 %collective-permute-done.7.refs_0_ = f32[7,8,2048]{2,1,0:T(8,128)S(1)} collective-permute-done((f32[7,8,2048]{2,1,0:T(8,128)S(1)}, f32[7,8,2048]{2,1,0:T(8,128)S(1)}, u32[]{:S(2)}, u32[]{:S(2)}) %collective-permute-start.7) | collective-permute-done | bytes 458784 | tf_op jit(solution)/shard_map/ppermute | solution.py:435
  84.0 0.7 combine_fields_3.3.inner_ref
  84.8 5.4 %collective-permute-done.13.src_after_ref = f32[4,8,2048]{2,1,0:T(8,128)S(1)} collective-permute-done((f32[4,8,2048]{2,1,0:T(8,128)S(1)}, f32[4,8,2048]{2,1,0:T(8,128)S(1)}, u32[]{:S(2)}, u32[]{:S(2)}) %collective-permute-start.13) | collective-permute-done | bytes 262176 | tf_op jit(solution)/shard_map/ppermute | solution.py:458
  90.2 2.0 %collective-permute-done.14.src_before_ref = f32[4,8,2048]{2,1,0:T(8,128)S(1)} collective-permute-done((f32[4,8,2048]{2,1,0:T(8,128)S(1)}, f32[4,8,2048]{2,1,0:T(8,128)S(1)}, u32[]{:S(2)}, u32[]{:S(2)}) %collective-permute-start.14) | collective-permute-done | bytes 262176 | tf_op jit(solution)/shard_map/ppermute | solution.py:459
  92.2 13.2 %final.1 = (f32[8,16,2048]{2,1,0:T(8,128)}, f32[8,16,2048]{2,1,0:T(8,128)}, f32[8,16,2048]{2,1,0:T(8,128)}) custom-call(f32[7,8,2048]{2,1,0:T(8,128)S(1)} %combine_fields_3.2.edge_ref, f32[7,8,2048]{2,1,0:T(8,128)S(1)} %combine_fields_3.3.inner_ref, f32[2,16,2048]{2,1,0:T(8,128)S(1)} %combine_turn_3.1.phi_ref, ...), custom_call_target="tpu_custom_call" | custom-call | tf_op jit(solution)/shard_map/final/pallas_call | solution.py:406
  (38 shorter events, 5.5 us)
Async XLA Ops:
  0.6 9.1 %copy-start = (f32[8,16,2048]{2,1,0:T(8,128)S(1)}, f32[8,16,2048]{2,1,0:T(8,128)}, u32[]{:S(2)}) copy-start(f32[8,16,2048]{2,1,0:T(8,128)} %e_hbm.1) | copy-start | bytes 3145732
  3.4 6.0 %collective-permute-start = (f32[16,2048]{1,0:T(8,128)S(1)}, f32[16,2048]{1,0:T(8,128)S(1)}, u32[]{:S(2)}, u32[]{:S(2)}) collective-permute-start(f32[16,2048]{1,0:T(8,128)S(1)} %pad_maximum_fusion), channel_id=1, source_target_pairs={{0,1},{1,2},{2,3},{3,4},{4,5},{5,6},{6,7},{7,0},{8,9},{9,10},{10,1... | collective-permute-start | bytes 393224 | tf_op jit(solution)/shard_map/ppermute | solution.py:431
  4.0 5.7 %collective-permute-start.1 = (f32[16,2048]{1,0:T(8,128)S(1)}, f32[16,2048]{1,0:T(8,128)S(1)}, u32[]{:S(2)}, u32[]{:S(2)}) collective-permute-start(f32[16,2048]{1,0:T(8,128)S(1)} %pad_maximum_fusion.1), channel_id=1, source_target_pairs={{1,0},{2,1},{3,2},{4,3},{5,4},{6,5},{7,6},{0,7},{9,8},{10,9},{11,1... | collective-permute-start | bytes 393224 | tf_op jit(solution)/shard_map/ppermute | solution.py:432
  9.7 1.2 %copy-start.1 = (f32[8,16,2048]{2,1,0:T(8,128)S(1)}, f32[8,16,2048]{2,1,0:T(8,128)}, u32[]{:S(2)}) copy-start(f32[8,16,2048]{2,1,0:T(8,128)} %n_hbm.1) | copy-start | bytes 3145732
  10.9 1.2 %copy-start.3 = (f32[8,16,2048]{2,1,0:T(8,128)S(1)}, f32[8,16,2048]{2,1,0:T(8,128)}, u32[]{:S(2)}) copy-start(f32[8,16,2048]{2,1,0:T(8,128)} %h_ref.1) | copy-start | bytes 3145732
  12.2 21.6 %copy-start.2 = (f32[8,16,2048]{2,1,0:T(8,128)S(1)}, f32[8,16,2048]{2,1,0:T(8,128)}, u32[]{:S(2)}) copy-start(f32[8,16,2048]{2,1,0:T(8,128)} %n_hbm.1) | copy-start | bytes 3145732
  14.5 1.0 copy-start.4
  15.4 0.7 copy-start.6
  16.1 0.7 copy-start.8
  16.8 14.5 %collective-permute-start.2 = (f32[7,8,2048]{2,1,0:T(8,128)S(1)}, f32[7,8,2048]{2,1,0:T(8,128)}, u32[]{:S(2)}, u32[]{:S(2)}) collective-permute-start(f32[7,8,2048]{2,1,0:T(8,128)S(1)} %get-tuple-element.22.refs_1_), channel_id=1, source_target_pairs={{0,8},{24,16},{1,9},{25,17},{2,10},{26,18},{3,11},{27,19},{4,12},{... | collective-permute-start | bytes 1376264 | tf_op jit(solution)/shard_map/ppermute | solution.py:435
  21.6 19.8 %collective-permute-start.5 = (f32[7,8,2048]{2,1,0:T(8,128)S(1)}, f32[7,8,2048]{2,1,0:T(8,128)S(1)}, u32[]{:S(2)}, u32[]{:S(2)}) collective-permute-start(f32[7,8,2048]{2,1,0:T(8,128)S(1)} %get-tuple-element.27.refs_1_), channel_id=1, source_target_pairs={{0,8},{24,16},{1,9},{25,17},{2,10},{26,18},{3,11},{27,19},{4,12},{... | collective-permute-start | bytes 1376264 | tf_op jit(solution)/shard_map/ppermute | solution.py:435
  33.0 15.8 %collective-permute-start.3 = (f32[7,8,2048]{2,1,0:T(8,128)S(1)}, f32[7,8,2048]{2,1,0:T(8,128)S(1)}, u32[]{:S(2)}, u32[]{:S(2)}) collective-permute-start(f32[7,8,2048]{2,1,0:T(8,128)S(1)} %get-tuple-element.23), channel_id=1, source_target_pairs={{8,16},{16,8},{9,17},{17,9},{10,18},{18,10},{11,19},{19,11},{12,20... | collective-permute-start | bytes 1376264 | tf_op jit(solution)/shard_map/ppermute | solution.py:435
  34.1 13.4 %collective-permute-start.8 = (f32[2,16,2048]{2,1,0:T(8,128)S(1)}, f32[2,16,2048]{2,1,0:T(8,128)S(1)}, u32[]{:S(2)}, u32[]{:S(2)}) collective-permute-start(f32[2,16,2048]{2,1,0:T(8,128)S(1)} %turn.1.refs_1_), channel_id=1, source_target_pairs={{0,8},{24,16},{1,9},{25,17},{2,10},{26,18},{3,11},{27,19},{4,12},{... | collective-permute-start | bytes 786440 | tf_op jit(solution)/shard_map/ppermute | solution.py:435
  42.5 10.6 %collective-permute-start.6 = (f32[7,8,2048]{2,1,0:T(8,128)S(1)}, f32[7,8,2048]{2,1,0:T(8,128)S(1)}, u32[]{:S(2)}, u32[]{:S(2)}) collective-permute-start(f32[7,8,2048]{2,1,0:T(8,128)S(1)} %get-tuple-element.28), channel_id=1, source_target_pairs={{8,16},{16,8},{9,17},{17,9},{10,18},{18,10},{11,19},{19,11},{12,20... | collective-permute-start | bytes 1376264 | tf_op jit(solution)/shard_map/ppermute | solution.py:435
  48.1 3.0 %collective-permute-start.9 = (f32[2,16,2048]{2,1,0:T(8,128)S(1)}, f32[2,16,2048]{2,1,0:T(8,128)S(1)}, u32[]{:S(2)}, u32[]{:S(2)}) collective-permute-start(f32[2,16,2048]{2,1,0:T(8,128)S(1)} %get-tuple-element.32), channel_id=1, source_target_pairs={{8,16},{16,8},{9,17},{17,9},{10,18},{18,10},{11,19},{19,11},{12,20... | collective-permute-start | bytes 786440 | tf_op jit(solution)/shard_map/ppermute | solution.py:435
  49.8 25.9 %collective-permute-start.4 = (f32[7,8,2048]{2,1,0:T(8,128)S(1)}, f32[7,8,2048]{2,1,0:T(8,128)S(1)}, u32[]{:S(2)}, u32[]{:S(2)}) collective-permute-start(f32[7,8,2048]{2,1,0:T(8,128)S(1)} %get-tuple-element.25), channel_id=1, source_target_pairs={{16,24},{8,0},{17,25},{9,1},{18,26},{10,2},{19,27},{11,3},{20,28},... | collective-permute-start | bytes 1376264 | tf_op jit(solution)/shard_map/ppermute | solution.py:435
  51.8 23.3 %collective-permute-start.10 = (f32[2,16,2048]{2,1,0:T(8,128)S(1)}, f32[2,16,2048]{2,1,0:T(8,128)S(1)}, u32[]{:S(2)}, u32[]{:S(2)}) collective-permute-start(f32[2,16,2048]{2,1,0:T(8,128)S(1)} %get-tuple-element.34), channel_id=1, source_target_pairs={{16,24},{8,0},{17,25},{9,1},{18,26},{10,2},{19,27},{11,3},{20,28},... | collective-permute-start | bytes 786440 | tf_op jit(solution)/shard_map/ppermute | solution.py:435
  54.2 29.9 %collective-permute-start.7 = (f32[7,8,2048]{2,1,0:T(8,128)S(1)}, f32[7,8,2048]{2,1,0:T(8,128)S(1)}, u32[]{:S(2)}, u32[]{:S(2)}) collective-permute-start(f32[7,8,2048]{2,1,0:T(8,128)S(1)} %get-tuple-element.30), channel_id=1, source_target_pairs={{16,24},{8,0},{17,25},{9,1},{18,26},{10,2},{19,27},{11,3},{20,28},... | collective-permute-start | bytes 1376264 | tf_op jit(solution)/shard_map/ppermute | solution.py:435
  76.5 1.0 copy-start.9
  76.5 2.9 %copy-start.7 = (f32[4,8,2048]{2,1,0:T(8,128)S(1)}, f32[4,8,2048]{2,1,0:T(8,128)}, u32[]{:S(2)}) copy-start(f32[4,8,2048]{2,1,0:T(8,128)} %copy-done.6) | copy-start | bytes 786436
  76.6 15.6 %copy-start.5 = (f32[8,16,2048]{2,1,0:T(8,128)S(1)}, f32[8,16,2048]{2,1,0:T(8,128)}, u32[]{:S(2)}) copy-start(f32[8,16,2048]{2,1,0:T(8,128)} %copy-done.4) | copy-start | bytes 3145732
  76.6 15.6 %collective-permute-start.11 = (f32[5,8,2048]{2,1,0:T(8,128)S(1)}, f32[5,8,2048]{2,1,0:T(8,128)S(1)}, u32[]{:S(2)}, u32[]{:S(2)}) collective-permute-start(f32[5,8,2048]{2,1,0:T(8,128)S(1)} %get-tuple-element.36), channel_id=1, source_target_pairs={{1,0},{2,1},{3,2},{4,3},{5,4},{6,5},{7,6},{0,7},{9,8},{10,9},{11,1... | collective-permute-start | bytes 983048 | tf_op jit(solution)/shard_map/ppermute | solution.py:474
  76.7 15.5 %collective-permute-start.12 = (f32[5,8,2048]{2,1,0:T(8,128)S(1)}, f32[5,8,2048]{2,1,0:T(8,128)S(1)}, u32[]{:S(2)}, u32[]{:S(2)}) collective-permute-start(f32[5,8,2048]{2,1,0:T(8,128)S(1)} %get-tuple-element.37), channel_id=1, source_target_pairs={{0,1},{1,2},{2,3},{3,4},{4,5},{5,6},{6,7},{7,0},{8,9},{9,10},{10,1... | collective-permute-start | bytes 983048 | tf_op jit(solution)/shard_map/ppermute | solution.py:475
  77.5 12.8 %collective-permute-start.13 = (f32[4,8,2048]{2,1,0:T(8,128)S(1)}, f32[4,8,2048]{2,1,0:T(8,128)S(1)}, u32[]{:S(2)}, u32[]{:S(2)}) collective-permute-start(f32[4,8,2048]{2,1,0:T(8,128)S(1)} %copy-done.9), channel_id=1, source_target_pairs={{1,0},{2,1},{3,2},{4,3},{5,4},{6,5},{7,6},{0,7},{9,8},{10,9},{11,1... | collective-permute-start | bytes 786440 | tf_op jit(solution)/shard_map/ppermute | solution.py:458
  79.4 12.8 %collective-permute-start.14 = (f32[4,8,2048]{2,1,0:T(8,128)S(1)}, f32[4,8,2048]{2,1,0:T(8,128)S(1)}, u32[]{:S(2)}, u32[]{:S(2)}) collective-permute-start(f32[4,8,2048]{2,1,0:T(8,128)S(1)} %copy-done.7), channel_id=1, source_target_pairs={{0,1},{1,2},{2,3},{3,4},{4,5},{5,6},{6,7},{7,0},{8,9},{9,10},{10,1... | collective-permute-start | bytes 786440 | tf_op jit(solution)/shard_map/ppermute | solution.py:459

commit v2 on v1

v2 whole, which is shorter than its diff:
```python
import functools
import math

import jax
import jax.numpy as jnp
import numpy as np
from jax import lax
from jax.experimental import pallas as pl
from jax.experimental.pallas import tpu as pltpu
from jax.sharding import PartitionSpec as P

alpha_window = 0.1
gravity = 1.0
mean_depth = 0.25
coriolis = 0.3
wave_speed = gravity * mean_depth
diagonal = 1.0 + coriolis * coriolis + 4.0 * wave_speed
turn_norm = 1.0 / (1.0 + coriolis * coriolis)
LANES = 128
MIB = 1 << 20


def step_matrix():
    m = np.zeros((7, 7))
    m[0, 0] = 1.0
    source = np.zeros(7)
    source[0] = coriolis
    for k in range(3):
        u, r = 1 + 2 * k, 2 + 2 * k
        new = source.copy()
        new[u] += 1.0
        new = new / diagonal
        m[r] = new
        m[u] = 2.0 * new
        m[u, r] -= 1.0
        source = wave_speed * new
    return m


def turn_matrix(value):
    return np.array([[np.real(value), -np.imag(value)], [np.imag(value), np.real(value)]])


def transitions(steps_local):
    spin = (1.0 / (1.0 + 1j * coriolis)) ** steps_local
    return np.linalg.matrix_power(step_matrix(), steps_local), turn_matrix(spin)


def message_weights(block, parts, hop):
    eye, power = np.eye(len(block)), np.linalg.matrix_power
    weights = [None] * parts
    weights[hop] = [block, eye]
    weights[parts - 1 - hop] = [eye, power(block, hop)]
    return weights


def arrival_weight(block, parts, b, hop):
    power = np.linalg.matrix_power
    closure = np.linalg.inv(np.eye(len(block)) - alpha_window * power(block, parts))
    if hop == 0:
        return alpha_window * closure @ power(block, parts - 1)
    if hop == b:
        return closure
    if hop == parts - 1 - b:
        return alpha_window * closure @ power(block, b)
    return None


def start_rows():
    one = step_matrix()
    inverse = np.linalg.inv((1.0 + 1j * coriolis) * one - np.eye(7))
    return [one[2 + 2 * k] @ inverse for k in range(3)]


def low_half(shape):
    return lax.broadcasted_iota(jnp.int32, shape, len(shape) - 2) < 4


def wide(load, start, width, total):
    left = pl.multiple_of(lax.rem(start + (total - LANES), total), LANES)
    right = pl.multiple_of(lax.rem(start + width, total), LANES)
    return jnp.concatenate(
        [load(pl.ds(left, LANES)), load(pl.ds(start, width)), load(pl.ds(right, LANES))], axis=-1
    )


def core(x):
    return x[:, LANES : x.shape[1] - LANES]


def next_column(x):
    return core(pltpu.roll(x, x.shape[1] - 1, 1))


def previous_column(x):
    return core(pltpu.roll(x, 1, 1))


def next_row(x):
    return pltpu.roll(x, x.shape[0] - 1, 0)


def previous_row(x):
    return pltpu.roll(x, 1, 0)


def dx(x):
    return 0.5 * (next_column(x) - previous_column(x))


def dy(x):
    return 0.5 * (next_row(x) - previous_row(x))


def turn_kernel(e_hbm, n_hbm, out_ref, prev_ref, next_ref, e_ref, n_ref, sems, *, width):
    steps, rows, total = e_ref.shape
    copies = []
    for step in range(0, steps, 2):
        part = pl.ds(step, 2)
        copies.append(pltpu.make_async_copy(e_hbm.at[part], e_ref.at[part], sems.at[step]))
        copies.append(pltpu.make_async_copy(n_hbm.at[part], n_ref.at[part], sems.at[step + 1]))
    for copy in copies:
        copy.start()
    for copy in copies:
        copy.wait()
    for step in range(steps):
        for ref, at in ((e_ref, step), (n_ref, steps + step)):
            prev_ref[at : at + 1, :] = ref[step, 0:1, :]
            next_ref[at : at + 1, :] = ref[step, rows - 1 : rows, :]

    def block(i, carry):
        cols = pl.ds(pl.multiple_of(i * width, width), width)
        re, im = e_ref[0, :, cols], n_ref[0, :, cols]
        re, im = turn_norm * (re + coriolis * im), turn_norm * (im - coriolis * re)
        for step in range(1, steps):
            re, im = re + e_ref[step, :, cols], im + n_ref[step, :, cols]
            re, im = turn_norm * (re + coriolis * im), turn_norm * (im - coriolis * re)
        out_ref[0, :, cols] = re
        out_ref[1, :, cols] = im
        return carry

    lax.fori_loop(0, total // width, block, 0)


def sublane(x):
    return lax.broadcasted_iota(jnp.int32, x.shape, 0)


def pack_rows(tiles, first):
    out = []
    for t in range(-(-3 * len(tiles) // 8)):
        packed = None
        for k, tile in enumerate(tiles):
            at = 3 * k - 8 * t
            if -3 < at < 8:
                moved = pltpu.roll(tile, (at - first) % 8, 0) if (at - first) % 8 else tile
                packed = moved if packed is None else jnp.where(sublane(tile) >= at, moved, packed)
        out.append(packed)
    return out


def unpack_rows(load, k, first):
    t = 3 * k // 8
    tile = load(t)
    at = 3 * k - 8 * t
    out = pltpu.roll(tile, (first - at) % 8, 0) if (first - at) % 8 else tile
    if at > 5:
        other = pltpu.roll(load(t + 1), (first - at) % 8, 0) if (first - at) % 8 else load(t + 1)
        out = jnp.where(sublane(tile) >= first + 8 - at, other, out)
    return out


def halo_tile(after, before, k):
    a, b = unpack_rows(after, k, 0), unpack_rows(before, k, 5)
    return jnp.where(sublane(a) < 4, a, b)


def source_kernel(
    h_ref, e_ref, n_ref, before_ref, after_ref, src_ref, prev_ref, next_ref, *states, parts, width
):
    steps, rows, total = h_ref.shape

    def block(start, edge, edge_cols, inner, inner_cols):
        cols = pl.ds(start, width)
        row = lax.broadcasted_iota(jnp.int32, (rows, width), 0)
        first, last = row == 0, row == rows - 1
        low = low_half((8, width))

        def slopes(ref, step, at):
            x = wide(lambda c: ref[step, :, c], start, width, total)
            mid = core(x)
            line = pl.ds(at + step, 1)
            up = jnp.where(last, after_ref[line, cols], next_row(mid))
            down = jnp.where(first, before_ref[line, cols], previous_row(mid))
            return dx(x), 0.5 * (up - down)

        p = jnp.zeros((rows, width), jnp.float32)
        state = [p] * 6
        edges = []
        h_last = None
        for step in range(steps):
            h = h_ref[step, :, cols]
            e_x, e_y = slopes(e_ref, step, 0)
            n_x, n_y = slopes(n_ref, step, steps)
            p = p + (coriolis * h - mean_depth * (n_x - e_y))
            change = h if h_last is None else h - h_last
            src = (change - mean_depth * (e_x + n_y)) + coriolis * p
            h_last = h
            src_ref[step, :, cols] = src
            top, bottom = src[:8], src[8:]
            edges.append(jnp.where(low, top, bottom))
            state = advance(src, state)
        for ref, first in ((prev_ref, 0), (next_ref, 5)):
            for t, tile in enumerate(pack_rows(edges, first)):
                ref[t, :, cols] = tile
        state[0] = state[0] - h_last
        for k, value in enumerate([p] + state):
            top, bottom = value[:8], value[8:]
            states[edge][k, :, edge_cols] = jnp.where(low, top, bottom)
            states[inner][k, :, inner_cols] = jnp.where(low, bottom, top)

    over_segments(parts, width, block)


def advance(source, state):
    out, x = [], source
    for k in range(3):
        u, r = state[2 * k], state[2 * k + 1]
        new = (x + u) * (1.0 / diagonal)
        out += [2.0 * new - r, new]
        x = wave_speed * new
    return out


def mix_kernel(*refs, weights, width):
    *args, out_ref = refs
    count, _, total = out_ref.shape
    me = lax.axis_index("tm")

    def run(matrices):
        def block(i, carry):
            cols = pl.ds(pl.multiple_of(i * width, width), width)
            sums = [None] * count
            for ref, matrix in zip(args, matrices):
                if matrix is None:
                    continue
                fields = [ref[k, :, cols] for k in range(count)]
                for k in range(count):
                    for j in range(count):
                        weight = float(np.float32(matrix[k, j]))
                        if weight != 0.0:
                            term = fields[j] if weight == 1.0 else weight * fields[j]
                            sums[k] = term if sums[k] is None else sums[k] + term
            for k in range(count):
                out_ref[k, :, cols] = sums[k]
            return carry

        lax.fori_loop(0, total // width, block, 0)

    for b, matrices in enumerate(weights):
        if matrices is not None:
            pl.when(me == b)(functools.partial(run, matrices))


def segments(total, bounds):
    cuts = sorted({x % total for x in bounds} | {total})

    def place(x):
        chunk = max(c for c in range(len(bounds) - 1) if bounds[c] <= x)
        return chunk, x - bounds[chunk]

    return [(a, b - a, place(a), place(total + a)) for a, b in zip(cuts[:-1], cuts[1:])]


def over_segments(parts, width, body):
    for start, size, (edge, edge_at), (inner, inner_at) in parts:

        def block(i, carry):
            at = [pl.multiple_of(x + i * width, LANES) for x in (start, edge_at, inner_at)]
            body(at[0], edge, pl.ds(at[1], width), inner, pl.ds(at[2], width))
            return carry

        lax.fori_loop(0, size // width, block, 0)


def pack_kernel(*refs, parts, width):
    *states, prev_ref, next_ref = refs

    def block(start, edge, there, *_):
        cols = pl.ds(start, width)
        tiles = [states[edge][k, :, there] for k in range(7)]
        for ref, first in ((prev_ref, 0), (next_ref, 5)):
            for t, tile in enumerate(pack_rows(tiles, first)):
                ref[t, :, cols] = tile

    over_segments(parts, width, block)


def pack_turn_kernel(src_prev_ref, src_next_ref, phi_ref, prev_ref, next_ref):
    count, _, total = src_prev_ref.shape
    low = low_half((8, total))
    prev_ref[:count] = src_prev_ref[...]
    next_ref[:count] = src_next_ref[...]
    prev_ref[count] = jnp.where(low, phi_ref[0, :8], pltpu.roll(phi_ref[1, :8], 4, 0))
    next_ref[count] = jnp.where(low, pltpu.roll(phi_ref[1, 8:], 4, 0), phi_ref[0, 8:])


def final_kernel(*refs, parts, width):
    count = 1 + max(inner for _, _, _, (inner, _) in parts)
    states, refs = refs[:count], refs[count:]
    (
        phi_ref, s_after_ref, s_before_ref, src_ref, src_after_ref, src_before_ref, e_hbm, n_hbm,
        h_out, e_out, n_out, r1, r2, r3, ring, e_ref, n_ref, u_ref, v_ref, sems,
    ) = refs
    steps, rows, total = src_ref.shape
    copies_in = [
        pltpu.make_async_copy(e_hbm, e_ref, sems.at[0]),
        pltpu.make_async_copy(n_hbm, n_ref, sems.at[1]),
    ]
    for copy in copies_in:
        copy.start()
    lines = [np.asarray(line) for line in start_rows()]

    def filters(start, edge_at, edge_cols, inner_at, inner_cols):
        cols = pl.ds(start, width)
        low = low_half((8, width))
        fields = []
        for k in range(7):
            edge, inner = states[edge_at][k, :, edge_cols], states[inner_at][k, :, inner_cols]
            halo = halo_tile(lambda t: s_after_ref[t, :, cols], lambda t: s_before_ref[t, :, cols], k)
            fields.append(
                jnp.concatenate([jnp.where(low, edge, inner), jnp.where(low, inner, edge), halo], 0)
            )
        turned_tile = src_after_ref.shape[0] - 1
        a, b = src_after_ref[turned_tile, :, cols], src_before_ref[turned_tile, :, cols]
        ring[0, :, cols] = jnp.concatenate([phi_ref[0, :, cols], jnp.where(low, a, b)], 0)
        ring[1, :, cols] = jnp.concatenate(
            [phi_ref[1, :, cols], pltpu.roll(jnp.where(low, b, a), 4, 0)], 0
        )
        for planes, line in ((r1, lines[0]), (r2, lines[1]), (r3, lines[2])):
            for part, weights in ((0, np.real(line)), (1, np.imag(line))):
                value = None
                for j in range(7):
                    if weights[j] != 0.0:
                        term = float(weights[j]) * fields[j]
                        value = term if value is None else value + term
                planes[steps + part, :, cols] = value
        turned = coriolis * fields[0]
        state = fields[1:]
        for step in range(steps):
            halo = halo_tile(lambda t: src_after_ref[t, :, cols], lambda t: src_before_ref[t, :, cols], step)
            source = jnp.concatenate([src_ref[step, :, cols], halo], 0) + turned
            state = advance(source, state)
            r1[step, :, cols] = state[1]
            r2[step, :, cols] = state[3]
            r3[step, :, cols] = state[5]

    over_segments(parts, width, filters)

    def row_dx(x):
        return 0.5 * (pltpu.roll(x, total - 1, 1) - pltpu.roll(x, 1, 1))

    def row_neighbours(x):
        return (next_row(x) + previous_row(x)) + (pltpu.roll(x, total - 1, 1) + pltpu.roll(x, 1, 1))

    re, im = ring[0], ring[1]
    chi = (row_dx(re) + dy(im), row_dx(im) - dy(re))
    share = mean_depth / (4.0 * wave_speed)
    for planes, part_share in ((r1, share), (r2, share / 4.0), (r3, share / 16.0)):
        for part in range(2):
            planes[steps + part] = planes[steps + part] - part_share * chi[part]
    for low_planes, high_planes in ((r2, r3), (r1, r2)):
        for k in range(steps + 2):
            low_planes[k] = low_planes[k] + row_neighbours(high_planes[k])
    height_copy = pltpu.make_async_copy(r1.at[pl.ds(0, steps), pl.ds(0, rows)], h_out, sems.at[2])
    height_copy.start()
    for copy in copies_in:
        copy.wait()

    def slopes(k):
        x = r1[k]
        return row_dx(x[:rows]), dy(x)[:rows]

    re_x, re_y = slopes(steps)
    im_x, im_y = slopes(steps + 1)
    u = ring[0, :rows] - gravity * (re_x - im_y)
    v = ring[1, :rows] - gravity * (im_x + re_y)
    copies_out = [height_copy]
    for step in range(steps):
        eta_x, eta_y = slopes(step)
        re = u + (e_ref[step] - gravity * eta_x)
        im = v + (n_ref[step] - gravity * eta_y)
        u, v = turn_norm * (re + coriolis * im), turn_norm * (im - coriolis * re)
        u_ref[step] = u
        v_ref[step] = v
        for ref, out, sem in ((u_ref, e_out, 3 + 2 * step), (v_ref, n_out, 4 + 2 * step)):
            copies_out.append(pltpu.make_async_copy(ref.at[step], out.at[step], sems.at[sem]))
            copies_out[-1].start()
    for copy in copies_out:
        copy.wait()


VMEM = pl.BlockSpec(memory_space=pltpu.VMEM)
ANY = pl.BlockSpec(memory_space=pl.ANY)


def f32(*shape):
    return jax.ShapeDtypeStruct(shape, jnp.float32)


def call(kernel, args, outs, name, in_specs=None, limit=16, scratch=(), out_specs=None, after=()):
    count = len(args)

    def run(*refs):
        kernel(*refs[:count], *refs[count + len(after) :])

    return pl.pallas_call(
        run,
        out_shape=outs,
        in_specs=(in_specs or [VMEM] * count) + [ANY] * len(after),
        out_specs=out_specs or [VMEM] * len(outs),
        scratch_shapes=scratch,
        compiler_params=pltpu.CompilerParams(vmem_limit_bytes=limit * MIB),
        cost_estimate=pl.CostEstimate(flops=COST, bytes_accessed=1000, transcendentals=0),
        name=name,
    )(*args, *after)


def shifts(axis):
    count = lax.axis_size(axis)
    forward = [(i, (i + 1) % count) for i in range(count)]
    return forward, [(t, s) for s, t in forward]


CHUNKS = 4
LAG = 1.01
FIN = 0.0
SINCE = 7
COST = 2 * 10**9


def body(h, e, n):
    steps, rows, total = h.shape
    parts = lax.axis_size("tm")
    unit = 256 if total % 256 == 0 and 2 * total >= 256 * CHUNKS else LANES
    bounds = [-(-2 * total // unit * i // CHUNKS) * unit for i in range(CHUNKS + 1)]
    places = segments(total, bounds)
    fields_block, turn_block = transitions(steps)
    forward, backward = shifts("space")

    def hop(x, k):
        return lax.ppermute(x, "tm", [(k - 1, k), (parts - k, parts - 1 - k)])

    def mix(args, weights, name, after):
        kernel = functools.partial(mix_kernel, weights=weights, width=unit)
        return call(kernel, args, [f32(*args[0].shape)], name, limit=8, after=after)[0]

    line = f32(2 * steps, total)
    whole = pltpu.VMEM((steps, rows, total), jnp.float32)
    phi, first_rows, last_rows = call(
        functools.partial(turn_kernel, width=unit), [e, n], [f32(2, rows, total), line, line], "turn",
        [ANY] * 2, scratch=[whole, whole, pltpu.SemaphoreType.DMA((steps,))],
    )
    before = lax.ppermute(last_rows, "space", forward)
    after = lax.ppermute(first_rows, "space", backward)
    src_tiles = -(-3 * steps // 8)
    pack = f32(src_tiles, 8, total)
    src, src_prev, src_next, *states = call(
        functools.partial(source_kernel, parts=places, width=2 * unit),
        [h, e, n, before, after],
        [f32(steps, rows, total), pack, pack] + [f32(7, 8, b - a) for a, b in zip(bounds[:-1], bounds[1:])],
        "source",
    )

    chunks = [(phi, turn_block)] + [(x, fields_block) for x in states]
    message = [own for own, _ in chunks]
    brought = [[] for _ in chunks]
    done = [None] * len(chunks)
    last_edge = 1 + max(edge for _, _, (edge, _), _ in places)
    latest, packs = states[0], None
    since = packs_sent = 0
    order = [(j, k) for j in range(len(chunks)) for k in range(1, parts)]
    for j, k in sorted(order, key=lambda jk: jk[0] + (jk[1] - 1) * LAG + FIN * (jk[1] == parts - 1)):
        own, block = chunks[j]
        deps = [latest]
        since += packs_sent
        if since == SINCE:
            deps += [src_after, src_before]
        brought[j].append(hop(message[j], k))
        if k < parts - 1:
            message[j] = mix([brought[j][-1], own], message_weights(block, parts, k), f"message_{j}_{k}", deps)
            latest = message[j]
        if k == max(parts - 2, 1):
            weights = [[arrival_weight(block, parts, b, i) for i in range(k + 1)] for b in range(parts)]
            done[j] = mix([own] + brought[j], weights, f"settle_{j}", [latest])
        if k == parts - 1 and k > 1:
            weights = [[np.eye(len(block)), arrival_weight(block, parts, b, k)] for b in range(parts)]
            done[j] = mix([done[j], brought[j][-1]], weights, f"finish_{j}", deps)
            latest = done[j]
        if k == parts - 1 and j == 0:
            src_prev, src_next = call(
                pack_turn_kernel, [src_prev, src_next, done[0]], [f32(src_tiles + 1, 8, total)] * 2, "pack_turn",
                limit=8,
            )
            src_after = lax.ppermute(src_prev, "space", backward)
            src_before = lax.ppermute(src_next, "space", forward)
            latest, packs_sent = src_prev, 1
        if k == parts - 1 and j == last_edge:
            packs = call(
                functools.partial(pack_kernel, parts=places, width=unit),
                done[1 : 1 + last_edge], [f32(3, 8, total)] * 2, "pack", limit=8,
            )
            latest = packs[0]
    to_prev, to_next = packs
    s_after = lax.ppermute(to_prev, "space", backward)
    s_before = lax.ppermute(to_next, "space", forward)

    planes = pltpu.VMEM((steps + 2, rows + 8, total), jnp.float32)
    return tuple(
        call(
            functools.partial(final_kernel, parts=places, width=unit),
            done[1:] + [done[0], s_after, s_before, src, src_after, src_before, e, n],
            [f32(steps, rows, total)] * 3,
            "final",
            [VMEM] * (CHUNKS + 6) + [ANY] * 2,
            24,
            [planes, planes, planes, pltpu.VMEM((2, rows + 8, total), jnp.float32)]
            + [whole] * 4
            + [pltpu.SemaphoreType.DMA((3 + 2 * steps,))],
            [ANY] * 3,
        )
    )


def solution(mesh):
    specs = (P("tm", "space", None),) * 3
    return jax.shard_map(body, mesh=mesh, in_specs=specs, out_specs=specs, check_vma=False)
```

time: 106 us -> 67.4 us (0.64)
  waiting for transfers between devices: 46.5 us -> 20.5 us
  Pallas kernels: 24.2 us -> 10.5 us
  starting transfers between devices: 25.2 us -> 32.4 us
  local copies, waits for them, and re-layouts: 8.6 us -> 2.46 us
    ppermute x9 -> x15, waiting for transfers between devices: 36.3 us -> 20.5 us  [hop(): return lax.ppermute(x, 'tm', [(k - 1, k), (parts - k, parts - 1 - k)])]
    pallas_call x13 -> x25, Pallas kernels: 24.2 us -> 10.5 us  [call(): pl.pallas_call(run, out_shape=outs, in_specs=(in_specs or [VMEM] * count)...]
    ppermute x9 -> x15, starting transfers between devices: 19.3 us -> 26.2 us  [hop(): return lax.ppermute(x, 'tm', [(k - 1, k), (parts - k, parts - 1 - k)])]
    ppermute x1, waiting for transfers between devices: 5.41 us -> 0.01 us  [body(): src_after = lax.ppermute(src_prev, 'space', backward)]
    ppermute x2, waiting for transfers between devices: 2.78 us -> 0.01 us  [the longest x1 0.01 us: body(): before = lax.ppermute(last_rows, 'space', forward)]
    slice x2 -> x0, local copies, waits for them, and re-layouts: 2.68 us -> none  [the longest x1 1.38 us: body(): e[:, 0]]
    unnamed x20 -> x10, local copies, waits for them, and re-layouts: 5.12 us -> 2.46 us
    ppermute x1, starting transfers between devices: 0.12 us -> 2.66 us  [body(): s_after = lax.ppermute(to_prev, 'space', backward)]
  transfers between devices with their start and end apart: 15 -> 21, of which waited for: 8 -> 6; matrix products, arithmetic and copies ran while one was open for 1% -> 0% of each run, Pallas kernels for 8% -> 6%
where the time goes in v2:
time: 67.4 us; the launch traced here: 66.9 us
  starting transfers between devices  32.4 us (48%)
  waiting for transfers between devices  20.5 us (30%)
  Pallas kernels  10.5 us (16%)
  local copies, waits for them, and re-layouts  2.46 us (4%)
  between operations  1.1 us (2%)
    ppermute x15, starting transfers between devices, hop(): return lax.ppermute(x, 'tm', [(k - 1, k), (parts - k, parts - 1 - k)])  26.2 us
    ppermute x15, waiting for transfers between devices, hop(): return lax.ppermute(x, 'tm', [(k - 1, k), (parts - k, parts - 1 - k)])  20.5 us
    pallas_call x25, Pallas kernels, call(): pl.pallas_call(run, out_shape=outs, in_specs=(in_specs or [VMEM] * count)...  10.5 us
    ppermute x1, starting transfers between devices, body(): after = lax.ppermute(first_rows, 'space', backward)  2.95 us
    ppermute x1, starting transfers between devices, body(): s_after = lax.ppermute(to_prev, 'space', backward)  2.66 us
    unnamed x10, local copies, waits for them, and re-layouts  2.46 us
  transfers between devices with their start and end apart: 21, of which 6 were waited for; matrix products, arithmetic and copies ran while one was open for 0% of the time, Pallas kernels for 6%

profile of v2, /device:TPU:0, one launch (start us, length us, event | category | flops | bytes accessed | tf_op | source)
XLA Modules:
  0.0 66.9 jit_solution(12785240900554148167)
XLA Ops:
  0.6 1.2 %copy-done.1 = f32[8,16,2048]{2,1,0:T(8,128)S(1)} copy-done((f32[8,16,2048]{2,1,0:T(8,128)S(1)}, f32[8,16,2048]{2,1,0:T(8,128)}, u32[]{:S(2)}) %copy-start.1) | copy-done | bytes 1048600
  1.9 1.2 %copy-done.3 = f32[8,16,2048]{2,1,0:T(8,128)S(1)} copy-done((f32[8,16,2048]{2,1,0:T(8,128)S(1)}, f32[8,16,2048]{2,1,0:T(8,128)}, u32[]{:S(2)}) %copy-start.3) | copy-done | bytes 1048600
  3.1 0.6 turn.1
  3.7 0.5 collective-permute-start
  4.2 2.9 %collective-permute-start.1 = (f32[16,2048]{1,0:T(8,128)S(1)}, f32[16,2048]{1,0:T(8,128)S(1)}, u32[]{:S(2)}, u32[]{:S(2)}) collective-permute-start(f32[16,2048]{1,0:T(8,128)S(1)} %get-tuple-element.18), channel_id=1, source_target_pairs={{1,0},{2,1},{3,2},{4,3},{5,4},{6,5},{7,6},{0,7},{9,8},{10,9},{11,1... | collective-permute-start | bytes 393224 | tf_op jit(solution)/shard_map/ppermute | solution.py:465
  7.2 4.2 %collective-permute-start.3 = (f32[2,16,2048]{2,1,0:T(8,128)S(1)}, f32[2,16,2048]{2,1,0:T(8,128)S(1)}, u32[]{:S(2)}, u32[]{:S(2)}) collective-permute-start(f32[2,16,2048]{2,1,0:T(8,128)S(1)} %get-tuple-element.20.refs_1_.refs_0_), channel_id=1, source_target_pairs={{0,8},{24,16},{1,9},{25,17},{2,10},{26,18},{3,11},{27,19},{4,12},{... | collective-permute-start | bytes 786440 | tf_op jit(solution)/shard_map/ppermute | solution.py:452
  11.4 2.3 %source.1 = (f32[8,16,2048]{2,1,0:T(8,128)S(1)}, f32[3,8,2048]{2,1,0:T(8,128)S(1)}, f32[3,8,2048]{2,1,0:T(8,128)S(1)}, f32[7,8,1024]{2,1,0:T(8,128)S(1)}, f32[7,...) custom-call(f32[8,16,2048]{2,1,0:T(8,128)S(1)} %copy-done, ...), custom_call_target="tpu_custom_call" | custom-call | flops 2000000000 | bytes 1000 | tf_op jit(solution)/shard_map/source/pallas_call | solution.py:417
  13.7 2.6 %collective-permute-start.2 = (f32[7,8,1024]{2,1,0:T(8,128)S(1)}, f32[7,8,1024]{2,1,0:T(8,128)S(1)}, u32[]{:S(2)}, u32[]{:S(2)}) collective-permute-start(f32[7,8,1024]{2,1,0:T(8,128)S(1)} %get-tuple-element.19.refs_2_.refs_1_.refs_0_), channel_id=1, source_target_pairs={{0,8},{24,16},{1,9},{25,17},{2,10},{26,18},{3,11},{27,19},{4,12},{... | collective-permute-start | bytes 688136 | tf_op jit(solution)/shard_map/ppermute | solution.py:452
  16.4 0.7 %collective-permute-start.6 = (f32[2,16,2048]{2,1,0:T(8,128)S(1)}, f32[2,16,2048]{2,1,0:T(8,128)S(1)}, u32[]{:S(2)}, u32[]{:S(2)}) collective-permute-start(f32[2,16,2048]{2,1,0:T(8,128)S(1)} %message_0_1.1.refs_2_), channel_id=1, source_target_pairs={{8,16},{16,8},{9,17},{17,9},{10,18},{18,10},{11,19},{19,11},{12,20... | collective-permute-start | bytes 786440 | tf_op jit(solution)/shard_map/ppermute | solution.py:452
  17.1 6.9 %collective-permute-start.5 = (f32[7,8,1024]{2,1,0:T(8,128)S(1)}, f32[7,8,1024]{2,1,0:T(8,128)S(1)}, u32[]{:S(2)}, u32[]{:S(2)}) collective-permute-start(f32[7,8,1024]{2,1,0:T(8,128)S(1)} %get-tuple-element.21.refs_1_.refs_0_), channel_id=1, source_target_pairs={{0,8},{24,16},{1,9},{25,17},{2,10},{26,18},{3,11},{27,19},{4,12},{... | collective-permute-start | bytes 688136 | tf_op jit(solution)/shard_map/ppermute | solution.py:452
  24.0 1.3 %collective-permute-start.9 = (f32[7,8,1024]{2,1,0:T(8,128)S(1)}, f32[7,8,1024]{2,1,0:T(8,128)S(1)}, u32[]{:S(2)}, u32[]{:S(2)}) collective-permute-start(f32[7,8,1024]{2,1,0:T(8,128)S(1)} %get-tuple-element.22.refs_1_.refs_0_), channel_id=1, source_target_pairs={{0,8},{24,16},{1,9},{25,17},{2,10},{26,18},{3,11},{27,19},{4,12},{... | collective-permute-start | bytes 688136 | tf_op jit(solution)/shard_map/ppermute | solution.py:452
  25.3 1.3 %collective-permute-start.13 = (f32[7,8,1024]{2,1,0:T(8,128)S(1)}, f32[7,8,1024]{2,1,0:T(8,128)S(1)}, u32[]{:S(2)}, u32[]{:S(2)}) collective-permute-start(f32[7,8,1024]{2,1,0:T(8,128)S(1)} %get-tuple-element.26.refs_1_.refs_0_), channel_id=1, source_target_pairs={{0,8},{24,16},{1,9},{25,17},{2,10},{26,18},{3,11},{27,19},{4,12},{... | collective-permute-start | bytes 688136 | tf_op jit(solution)/shard_map/ppermute | solution.py:452
  26.7 0.7 %collective-permute-start.4 = (f32[7,8,1024]{2,1,0:T(8,128)S(1)}, f32[7,8,1024]{2,1,0:T(8,128)S(1)}, u32[]{:S(2)}, u32[]{:S(2)}) collective-permute-start(f32[7,8,1024]{2,1,0:T(8,128)S(1)} %message_1_1.1.refs_2_), channel_id=1, source_target_pairs={{8,16},{16,8},{9,17},{17,9},{10,18},{18,10},{11,19},{19,11},{12,20... | collective-permute-start | bytes 688136 | tf_op jit(solution)/shard_map/ppermute | solution.py:452
  27.4 1.3 %collective-permute-start.10 = (f32[2,16,2048]{2,1,0:T(8,128)S(1)}, f32[2,16,2048]{2,1,0:T(8,128)S(1)}, u32[]{:S(2)}, u32[]{:S(2)}) collective-permute-start(f32[2,16,2048]{2,1,0:T(8,128)S(1)} %message_0_2.1.refs_2_.refs_3_), channel_id=1, source_target_pairs={{16,24},{8,0},{17,25},{9,1},{18,26},{10,2},{19,27},{11,3},{20,28},... | collective-permute-start | bytes 786440 | tf_op jit(solution)/shard_map/ppermute | solution.py:452
  28.7 1.3 %collective-permute-done.5.refs_0_.refs_1_ = f32[7,8,1024]{2,1,0:T(8,128)S(1)} collective-permute-done((f32[7,8,1024]{2,1,0:T(8,128)S(1)}, f32[7,8,1024]{2,1,0:T(8,128)S(1)}, u32[]{:S(2)}, u32[]{:S(2)}) %collective-permute-start.5) | collective-permute-done | bytes 229408 | tf_op jit(solution)/shard_map/ppermute | solution.py:452
  30.0 0.7 collective-permute-start.8
  30.9 1.3 %collective-permute-start.7 = (f32[7,8,1024]{2,1,0:T(8,128)S(1)}, f32[7,8,1024]{2,1,0:T(8,128)S(1)}, u32[]{:S(2)}, u32[]{:S(2)}) collective-permute-start(f32[7,8,1024]{2,1,0:T(8,128)S(1)} %message_1_2.1.refs_3_.refs_2_), channel_id=1, source_target_pairs={{16,24},{8,0},{17,25},{9,1},{18,26},{10,2},{19,27},{11,3},{20,28},... | collective-permute-start | bytes 688136 | tf_op jit(solution)/shard_map/ppermute | solution.py:452
  32.2 0.1 settle_1.1.refs_0_
  32.3 4.9 %collective-permute-done.10.refs_1_ = f32[2,16,2048]{2,1,0:T(8,128)S(1)} collective-permute-done((f32[2,16,2048]{2,1,0:T(8,128)S(1)}, f32[2,16,2048]{2,1,0:T(8,128)S(1)}, u32[]{:S(2)}, u32[]{:S(2)}) %collective-permute-start.10) | collective-permute-done | bytes 262176 | tf_op jit(solution)/shard_map/ppermute | solution.py:452
  37.5 0.7 %collective-permute-start.12 = (f32[7,8,1024]{2,1,0:T(8,128)S(1)}, f32[7,8,1024]{2,1,0:T(8,128)S(1)}, u32[]{:S(2)}, u32[]{:S(2)}) collective-permute-start(f32[7,8,1024]{2,1,0:T(8,128)S(1)} %message_3_1.1.refs_2_), channel_id=1, source_target_pairs={{8,16},{16,8},{9,17},{17,9},{10,18},{18,10},{11,19},{19,11},{12,20... | collective-permute-start | bytes 688136 | tf_op jit(solution)/shard_map/ppermute | solution.py:452
  38.2 1.3 %collective-permute-start.11 = (f32[7,8,1024]{2,1,0:T(8,128)S(1)}, f32[7,8,1024]{2,1,0:T(8,128)S(1)}, u32[]{:S(2)}, u32[]{:S(2)}) collective-permute-start(f32[7,8,1024]{2,1,0:T(8,128)S(1)} %message_2_2.1.refs_2_.refs_3_), channel_id=1, source_target_pairs={{16,24},{8,0},{17,25},{9,1},{18,26},{10,2},{19,27},{11,3},{20,28},... | collective-permute-start | bytes 688136 | tf_op jit(solution)/shard_map/ppermute | solution.py:452
  39.5 0.1 settle_2.1.refs_0_
  39.6 1.4 %collective-permute-done.7.refs_1_ = f32[7,8,1024]{2,1,0:T(8,128)S(1)} collective-permute-done((f32[7,8,1024]{2,1,0:T(8,128)S(1)}, f32[7,8,1024]{2,1,0:T(8,128)S(1)}, u32[]{:S(2)}, u32[]{:S(2)}) %collective-permute-start.7) | collective-permute-done | bytes 229408 | tf_op jit(solution)/shard_map/ppermute | solution.py:452
  41.2 0.7 %collective-permute-start.15 = (f32[7,8,1024]{2,1,0:T(8,128)S(1)}, f32[7,8,1024]{2,1,0:T(8,128)S(1)}, u32[]{:S(2)}, u32[]{:S(2)}) collective-permute-start(f32[7,8,1024]{2,1,0:T(8,128)S(1)} %message_4_1.1.refs_2_), channel_id=1, source_target_pairs={{8,16},{16,8},{9,17},{17,9},{10,18},{18,10},{11,19},{19,11},{12,20... | collective-permute-start | bytes 688136 | tf_op jit(solution)/shard_map/ppermute | solution.py:452
  41.9 1.3 %collective-permute-start.14 = (f32[7,8,1024]{2,1,0:T(8,128)S(1)}, f32[7,8,1024]{2,1,0:T(8,128)S(1)}, u32[]{:S(2)}, u32[]{:S(2)}) collective-permute-start(f32[7,8,1024]{2,1,0:T(8,128)S(1)} %message_3_2.1.refs_2_.refs_3_), channel_id=1, source_target_pairs={{16,24},{8,0},{17,25},{9,1},{18,26},{10,2},{19,27},{11,3},{20,28},... | collective-permute-start | bytes 688136 | tf_op jit(solution)/shard_map/ppermute | solution.py:452
  43.2 5.1 %collective-permute-done.11.refs_1_ = f32[7,8,1024]{2,1,0:T(8,128)S(1)} collective-permute-done((f32[7,8,1024]{2,1,0:T(8,128)S(1)}, f32[7,8,1024]{2,1,0:T(8,128)S(1)}, u32[]{:S(2)}, u32[]{:S(2)}) %collective-permute-start.11) | collective-permute-done | bytes 229408 | tf_op jit(solution)/shard_map/ppermute | solution.py:452
  48.5 0.1 settle_3.1.refs_0_
  48.7 2.7 %collective-permute-start.19 = (f32[3,8,2048]{2,1,0:T(8,128)S(1)}, f32[3,8,2048]{2,1,0:T(8,128)S(1)}, u32[]{:S(2)}, u32[]{:S(2)}) collective-permute-start(f32[3,8,2048]{2,1,0:T(8,128)S(1)} %get-tuple-element.27.refs_2_), channel_id=1, source_target_pairs={{1,0},{2,1},{3,2},{4,3},{5,4},{6,5},{7,6},{0,7},{9,8},{10,9},{11,1... | collective-permute-start | bytes 589832 | tf_op jit(solution)/shard_map/ppermute | solution.py:515
  51.3 1.3 %collective-permute-start.18 = (f32[7,8,1024]{2,1,0:T(8,128)S(1)}, f32[7,8,1024]{2,1,0:T(8,128)S(1)}, u32[]{:S(2)}, u32[]{:S(2)}) collective-permute-start(f32[7,8,1024]{2,1,0:T(8,128)S(1)} %message_4_2.1.refs_2_.refs_3_), channel_id=1, source_target_pairs={{16,24},{8,0},{17,25},{9,1},{18,26},{10,2},{19,27},{11,3},{20,28},... | collective-permute-start | bytes 688136 | tf_op jit(solution)/shard_map/ppermute | solution.py:452
  52.8 1.2 %collective-permute-done.14.refs_1_ = f32[7,8,1024]{2,1,0:T(8,128)S(1)} collective-permute-done((f32[7,8,1024]{2,1,0:T(8,128)S(1)}, f32[7,8,1024]{2,1,0:T(8,128)S(1)}, u32[]{:S(2)}, u32[]{:S(2)}) %collective-permute-start.14) | collective-permute-done | bytes 229408 | tf_op jit(solution)/shard_map/ppermute | solution.py:452
  54.1 6.6 %collective-permute-done.18.refs_1_ = f32[7,8,1024]{2,1,0:T(8,128)S(1)} collective-permute-done((f32[7,8,1024]{2,1,0:T(8,128)S(1)}, f32[7,8,1024]{2,1,0:T(8,128)S(1)}, u32[]{:S(2)}, u32[]{:S(2)}) %collective-permute-start.18) | collective-permute-done | bytes 229408 | tf_op jit(solution)/shard_map/ppermute | solution.py:452
  60.9 6.1 %final.1 = (f32[8,16,2048]{2,1,0:T(8,128)}, f32[8,16,2048]{2,1,0:T(8,128)}, f32[8,16,2048]{2,1,0:T(8,128)}) custom-call(f32[7,8,1024]{2,1,0:T(8,128)S(1)} %finish_1.1.refs_2_.refs_0_, f32[7,8,1024]{2,1,0:T(8,128)S(1)} %finish_2.1.refs_1_, f32[7,8,1024]{2,1,0:T(8,128)S(1)} %finish_3.1.refs_2_, f32[7,8,1024]{2,1,0:T(8,128)S(1)} %finish_4.1.refs_3_, ...), custom_call_target="tpu_custom_call" | custom-call | flops 2000000000 | bytes 1000 | tf_op jit(solution)/shard_map/final/pallas_call | solution.py:417
  (45 shorter events, 1.3 us)
Async XLA Ops:
  0.6 1.2 %copy-start.1 = (f32[8,16,2048]{2,1,0:T(8,128)S(1)}, f32[8,16,2048]{2,1,0:T(8,128)}, u32[]{:S(2)}) copy-start(f32[8,16,2048]{2,1,0:T(8,128)} %refs_10_.1) | copy-start | bytes 3145732
  1.9 1.2 %copy-start.3 = (f32[8,16,2048]{2,1,0:T(8,128)S(1)}, f32[8,16,2048]{2,1,0:T(8,128)}, u32[]{:S(2)}) copy-start(f32[8,16,2048]{2,1,0:T(8,128)} %refs_11_.1) | copy-start | bytes 3145732
  3.1 8.3 %copy-start = (f32[8,16,2048]{2,1,0:T(8,128)S(1)}, f32[8,16,2048]{2,1,0:T(8,128)}, u32[]{:S(2)}) copy-start(f32[8,16,2048]{2,1,0:T(8,128)} %refs_0_.3) | copy-start | bytes 3145732
  3.7 7.6 %collective-permute-start = (f32[16,2048]{1,0:T(8,128)S(1)}, f32[16,2048]{1,0:T(8,128)S(1)}, u32[]{:S(2)}, u32[]{:S(2)}) collective-permute-start(f32[16,2048]{1,0:T(8,128)S(1)} %get-tuple-element.17), channel_id=1, source_target_pairs={{0,1},{1,2},{2,3},{3,4},{4,5},{5,6},{6,7},{7,0},{8,9},{9,10},{10,1... | collective-permute-start | bytes 393224 | tf_op jit(solution)/shard_map/ppermute | solution.py:464
  4.2 7.1 %collective-permute-start.1 = (f32[16,2048]{1,0:T(8,128)S(1)}, f32[16,2048]{1,0:T(8,128)S(1)}, u32[]{:S(2)}, u32[]{:S(2)}) collective-permute-start(f32[16,2048]{1,0:T(8,128)S(1)} %get-tuple-element.18), channel_id=1, source_target_pairs={{1,0},{2,1},{3,2},{4,3},{5,4},{6,5},{7,6},{0,7},{9,8},{10,9},{11,1... | collective-permute-start | bytes 393224 | tf_op jit(solution)/shard_map/ppermute | solution.py:465
  7.2 9.2 %collective-permute-start.3 = (f32[2,16,2048]{2,1,0:T(8,128)S(1)}, f32[2,16,2048]{2,1,0:T(8,128)S(1)}, u32[]{:S(2)}, u32[]{:S(2)}) collective-permute-start(f32[2,16,2048]{2,1,0:T(8,128)S(1)} %get-tuple-element.20.refs_1_.refs_0_), channel_id=1, source_target_pairs={{0,8},{24,16},{1,9},{25,17},{2,10},{26,18},{3,11},{27,19},{4,12},{... | collective-permute-start | bytes 786440 | tf_op jit(solution)/shard_map/ppermute | solution.py:452
  13.7 12.9 %collective-permute-start.2 = (f32[7,8,1024]{2,1,0:T(8,128)S(1)}, f32[7,8,1024]{2,1,0:T(8,128)S(1)}, u32[]{:S(2)}, u32[]{:S(2)}) collective-permute-start(f32[7,8,1024]{2,1,0:T(8,128)S(1)} %get-tuple-element.19.refs_2_.refs_1_.refs_0_), channel_id=1, source_target_pairs={{0,8},{24,16},{1,9},{25,17},{2,10},{26,18},{3,11},{27,19},{4,12},{... | collective-permute-start | bytes 688136 | tf_op jit(solution)/shard_map/ppermute | solution.py:452
  16.4 11.0 %collective-permute-start.6 = (f32[2,16,2048]{2,1,0:T(8,128)S(1)}, f32[2,16,2048]{2,1,0:T(8,128)S(1)}, u32[]{:S(2)}, u32[]{:S(2)}) collective-permute-start(f32[2,16,2048]{2,1,0:T(8,128)S(1)} %message_0_1.1.refs_2_), channel_id=1, source_target_pairs={{8,16},{16,8},{9,17},{17,9},{10,18},{18,10},{11,19},{19,11},{12,20... | collective-permute-start | bytes 786440 | tf_op jit(solution)/shard_map/ppermute | solution.py:452
  17.1 13.0 %collective-permute-start.5 = (f32[7,8,1024]{2,1,0:T(8,128)S(1)}, f32[7,8,1024]{2,1,0:T(8,128)S(1)}, u32[]{:S(2)}, u32[]{:S(2)}) collective-permute-start(f32[7,8,1024]{2,1,0:T(8,128)S(1)} %get-tuple-element.21.refs_1_.refs_0_), channel_id=1, source_target_pairs={{0,8},{24,16},{1,9},{25,17},{2,10},{26,18},{3,11},{27,19},{4,12},{... | collective-permute-start | bytes 688136 | tf_op jit(solution)/shard_map/ppermute | solution.py:452
  24.0 13.4 %collective-permute-start.9 = (f32[7,8,1024]{2,1,0:T(8,128)S(1)}, f32[7,8,1024]{2,1,0:T(8,128)S(1)}, u32[]{:S(2)}, u32[]{:S(2)}) collective-permute-start(f32[7,8,1024]{2,1,0:T(8,128)S(1)} %get-tuple-element.22.refs_1_.refs_0_), channel_id=1, source_target_pairs={{0,8},{24,16},{1,9},{25,17},{2,10},{26,18},{3,11},{27,19},{4,12},{... | collective-permute-start | bytes 688136 | tf_op jit(solution)/shard_map/ppermute | solution.py:452
  25.3 15.8 %collective-permute-start.13 = (f32[7,8,1024]{2,1,0:T(8,128)S(1)}, f32[7,8,1024]{2,1,0:T(8,128)S(1)}, u32[]{:S(2)}, u32[]{:S(2)}) collective-permute-start(f32[7,8,1024]{2,1,0:T(8,128)S(1)} %get-tuple-element.26.refs_1_.refs_0_), channel_id=1, source_target_pairs={{0,8},{24,16},{1,9},{25,17},{2,10},{26,18},{3,11},{27,19},{4,12},{... | collective-permute-start | bytes 688136 | tf_op jit(solution)/shard_map/ppermute | solution.py:452
  26.7 4.2 %collective-permute-start.4 = (f32[7,8,1024]{2,1,0:T(8,128)S(1)}, f32[7,8,1024]{2,1,0:T(8,128)S(1)}, u32[]{:S(2)}, u32[]{:S(2)}) collective-permute-start(f32[7,8,1024]{2,1,0:T(8,128)S(1)} %message_1_1.1.refs_2_), channel_id=1, source_target_pairs={{8,16},{16,8},{9,17},{17,9},{10,18},{18,10},{11,19},{19,11},{12,20... | collective-permute-start | bytes 688136 | tf_op jit(solution)/shard_map/ppermute | solution.py:452
  27.4 9.8 %collective-permute-start.10 = (f32[2,16,2048]{2,1,0:T(8,128)S(1)}, f32[2,16,2048]{2,1,0:T(8,128)S(1)}, u32[]{:S(2)}, u32[]{:S(2)}) collective-permute-start(f32[2,16,2048]{2,1,0:T(8,128)S(1)} %message_0_2.1.refs_2_.refs_3_), channel_id=1, source_target_pairs={{16,24},{8,0},{17,25},{9,1},{18,26},{10,2},{19,27},{11,3},{20,28},... | collective-permute-start | bytes 786440 | tf_op jit(solution)/shard_map/ppermute | solution.py:452
  30.0 8.1 %collective-permute-start.8 = (f32[7,8,1024]{2,1,0:T(8,128)S(1)}, f32[7,8,1024]{2,1,0:T(8,128)S(1)}, u32[]{:S(2)}, u32[]{:S(2)}) collective-permute-start(f32[7,8,1024]{2,1,0:T(8,128)S(1)} %message_2_1.1.refs_2_), channel_id=1, source_target_pairs={{8,16},{16,8},{9,17},{17,9},{10,18},{18,10},{11,19},{19,11},{12,20... | collective-permute-start | bytes 688136 | tf_op jit(solution)/shard_map/ppermute | solution.py:452
  30.9 10.1 %collective-permute-start.7 = (f32[7,8,1024]{2,1,0:T(8,128)S(1)}, f32[7,8,1024]{2,1,0:T(8,128)S(1)}, u32[]{:S(2)}, u32[]{:S(2)}) collective-permute-start(f32[7,8,1024]{2,1,0:T(8,128)S(1)} %message_1_2.1.refs_3_.refs_2_), channel_id=1, source_target_pairs={{16,24},{8,0},{17,25},{9,1},{18,26},{10,2},{19,27},{11,3},{20,28},... | collective-permute-start | bytes 688136 | tf_op jit(solution)/shard_map/ppermute | solution.py:452
  37.4 14.0 %collective-permute-start.16 = (f32[4,8,2048]{2,1,0:T(8,128)S(1)}, f32[4,8,2048]{2,1,0:T(8,128)S(1)}, u32[]{:S(2)}, u32[]{:S(2)}) collective-permute-start(f32[4,8,2048]{2,1,0:T(8,128)S(1)} %get-tuple-element.25.refs_2_), channel_id=1, source_target_pairs={{1,0},{2,1},{3,2},{4,3},{5,4},{6,5},{7,6},{0,7},{9,8},{10,9},{11,1... | collective-permute-start | bytes 786440 | tf_op jit(solution)/shard_map/ppermute | solution.py:505
  37.5 4.4 %collective-permute-start.12 = (f32[7,8,1024]{2,1,0:T(8,128)S(1)}, f32[7,8,1024]{2,1,0:T(8,128)S(1)}, u32[]{:S(2)}, u32[]{:S(2)}) collective-permute-start(f32[7,8,1024]{2,1,0:T(8,128)S(1)} %message_3_1.1.refs_2_), channel_id=1, source_target_pairs={{8,16},{16,8},{9,17},{17,9},{10,18},{18,10},{11,19},{19,11},{12,20... | collective-permute-start | bytes 688136 | tf_op jit(solution)/shard_map/ppermute | solution.py:452
  38.2 10.1 %collective-permute-start.11 = (f32[7,8,1024]{2,1,0:T(8,128)S(1)}, f32[7,8,1024]{2,1,0:T(8,128)S(1)}, u32[]{:S(2)}, u32[]{:S(2)}) collective-permute-start(f32[7,8,1024]{2,1,0:T(8,128)S(1)} %message_2_2.1.refs_2_.refs_3_), channel_id=1, source_target_pairs={{16,24},{8,0},{17,25},{9,1},{18,26},{10,2},{19,27},{11,3},{20,28},... | collective-permute-start | bytes 688136 | tf_op jit(solution)/shard_map/ppermute | solution.py:452
  41.0 10.3 %collective-permute-start.17 = (f32[4,8,2048]{2,1,0:T(8,128)S(1)}, f32[4,8,2048]{2,1,0:T(8,128)S(1)}, u32[]{:S(2)}, u32[]{:S(2)}) collective-permute-start(f32[4,8,2048]{2,1,0:T(8,128)S(1)} %get-tuple-element.28), channel_id=1, source_target_pairs={{0,1},{1,2},{2,3},{3,4},{4,5},{5,6},{6,7},{7,0},{8,9},{9,10},{10,1... | collective-permute-start | bytes 786440 | tf_op jit(solution)/shard_map/ppermute | solution.py:506
  41.2 7.5 %collective-permute-start.15 = (f32[7,8,1024]{2,1,0:T(8,128)S(1)}, f32[7,8,1024]{2,1,0:T(8,128)S(1)}, u32[]{:S(2)}, u32[]{:S(2)}) collective-permute-start(f32[7,8,1024]{2,1,0:T(8,128)S(1)} %message_4_1.1.refs_2_), channel_id=1, source_target_pairs={{8,16},{16,8},{9,17},{17,9},{10,18},{18,10},{11,19},{19,11},{12,20... | collective-permute-start | bytes 688136 | tf_op jit(solution)/shard_map/ppermute | solution.py:452
  41.9 12.1 %collective-permute-start.14 = (f32[7,8,1024]{2,1,0:T(8,128)S(1)}, f32[7,8,1024]{2,1,0:T(8,128)S(1)}, u32[]{:S(2)}, u32[]{:S(2)}) collective-permute-start(f32[7,8,1024]{2,1,0:T(8,128)S(1)} %message_3_2.1.refs_2_.refs_3_), channel_id=1, source_target_pairs={{16,24},{8,0},{17,25},{9,1},{18,26},{10,2},{19,27},{11,3},{20,28},... | collective-permute-start | bytes 688136 | tf_op jit(solution)/shard_map/ppermute | solution.py:452
  48.5 12.3 %collective-permute-start.20 = (f32[3,8,2048]{2,1,0:T(8,128)S(1)}, f32[3,8,2048]{2,1,0:T(8,128)S(1)}, u32[]{:S(2)}, u32[]{:S(2)}) collective-permute-start(f32[3,8,2048]{2,1,0:T(8,128)S(1)} %get-tuple-element.29), channel_id=1, source_target_pairs={{0,1},{1,2},{2,3},{3,4},{4,5},{5,6},{6,7},{7,0},{8,9},{9,10},{10,1... | collective-permute-start | bytes 589832 | tf_op jit(solution)/shard_map/ppermute | solution.py:516
  48.7 12.2 %collective-permute-start.19 = (f32[3,8,2048]{2,1,0:T(8,128)S(1)}, f32[3,8,2048]{2,1,0:T(8,128)S(1)}, u32[]{:S(2)}, u32[]{:S(2)}) collective-permute-start(f32[3,8,2048]{2,1,0:T(8,128)S(1)} %get-tuple-element.27.refs_2_), channel_id=1, source_target_pairs={{1,0},{2,1},{3,2},{4,3},{5,4},{6,5},{7,6},{0,7},{9,8},{10,9},{11,1... | collective-permute-start | bytes 589832 | tf_op jit(solution)/shard_map/ppermute | solution.py:515
  51.3 9.3 %collective-permute-start.18 = (f32[7,8,1024]{2,1,0:T(8,128)S(1)}, f32[7,8,1024]{2,1,0:T(8,128)S(1)}, u32[]{:S(2)}, u32[]{:S(2)}) collective-permute-start(f32[7,8,1024]{2,1,0:T(8,128)S(1)} %message_4_2.1.refs_2_.refs_3_), channel_id=1, source_target_pairs={{16,24},{8,0},{17,25},{9,1},{18,26},{10,2},{19,27},{11,3},{20,28},... | collective-permute-start | bytes 688136 | tf_op jit(solution)/shard_map/ppermute | solution.py:452
  54.1 6.8 %copy-start.2 = (f32[8,16,2048]{2,1,0:T(8,128)S(1)}, f32[8,16,2048]{2,1,0:T(8,128)}, u32[]{:S(2)}) copy-start(f32[8,16,2048]{2,1,0:T(8,128)} %refs_10_.1) | copy-start | bytes 3145732
  54.1 6.8 %copy-start.4 = (f32[8,16,2048]{2,1,0:T(8,128)S(1)}, f32[8,16,2048]{2,1,0:T(8,128)}, u32[]{:S(2)}) copy-start(f32[8,16,2048]{2,1,0:T(8,128)} %refs_11_.1) | copy-start | bytes 3145732

commit v3 on v2

--- a/solution.py
+++ b/solution.py
@@ -408,7 +408,7 @@
     return jax.ShapeDtypeStruct(shape, jnp.float32)
 
 
-def call(kernel, args, outs, name, in_specs=None, limit=16, scratch=(), out_specs=None, after=()):
+def call(kernel, args, outs, name, in_specs=None, limit=16, scratch=(), out_specs=None, after=(), flops=None):
     count = len(args)
 
     def run(*refs):
@@ -421,7 +421,7 @@
         out_specs=out_specs or [VMEM] * len(outs),
         scratch_shapes=scratch,
         compiler_params=pltpu.CompilerParams(vmem_limit_bytes=limit * MIB),
-        cost_estimate=pl.CostEstimate(flops=COST, bytes_accessed=1000, transcendentals=0),
+        cost_estimate=pl.CostEstimate(flops=COST if flops is None else flops, bytes_accessed=1000, transcendentals=0),
         name=name,
     )(*args, *after)
 
@@ -434,9 +434,10 @@
 
 CHUNKS = 4
 LAG = 1.01
-FIN = 0.0
-SINCE = 7
-COST = 2 * 10**9
+SETTLE = 0
+FINISH = 0
+SINCE = 8
+COST = 25 * 10**8
 
 
 def body(h, e, n):
@@ -445,15 +446,16 @@
     unit = 256 if total % 256 == 0 and 2 * total >= 256 * CHUNKS else LANES
     bounds = [-(-2 * total // unit * i // CHUNKS) * unit for i in range(CHUNKS + 1)]
     places = segments(total, bounds)
+    span = math.gcd(4 * unit, *(size for _, size, _, _ in places))
     fields_block, turn_block = transitions(steps)
     forward, backward = shifts("space")
 
     def hop(x, k):
         return lax.ppermute(x, "tm", [(k - 1, k), (parts - k, parts - 1 - k)])
 
-    def mix(args, weights, name, after):
+    def mix(args, weights, name, after, flops=None):
         kernel = functools.partial(mix_kernel, weights=weights, width=unit)
-        return call(kernel, args, [f32(*args[0].shape)], name, limit=8, after=after)[0]
+        return call(kernel, args, [f32(*args[0].shape)], name, limit=8, after=after, flops=flops)[0]
 
     line = f32(2 * steps, total)
     whole = pltpu.VMEM((steps, rows, total), jnp.float32)
@@ -466,7 +468,7 @@
     src_tiles = -(-3 * steps // 8)
     pack = f32(src_tiles, 8, total)
     src, src_prev, src_next, *states = call(
-        functools.partial(source_kernel, parts=places, width=2 * unit),
+        functools.partial(source_kernel, parts=places, width=min(span, 2 * unit)),
         [h, e, n, before, after],
         [f32(steps, rows, total), pack, pack] + [f32(7, 8, b - a) for a, b in zip(bounds[:-1], bounds[1:])],
         "source",
@@ -480,7 +482,7 @@
     latest, packs = states[0], None
     since = packs_sent = 0
     order = [(j, k) for j in range(len(chunks)) for k in range(1, parts)]
-    for j, k in sorted(order, key=lambda jk: jk[0] + (jk[1] - 1) * LAG + FIN * (jk[1] == parts - 1)):
+    for j, k in sorted(order, key=lambda jk: jk[0] + (jk[1] - 1) * LAG):
         own, block = chunks[j]
         deps = [latest]
         since += packs_sent
@@ -492,10 +494,10 @@
             latest = message[j]
         if k == max(parts - 2, 1):
             weights = [[arrival_weight(block, parts, b, i) for i in range(k + 1)] for b in range(parts)]
-            done[j] = mix([own] + brought[j], weights, f"settle_{j}", [latest])
+            done[j] = mix([own] + brought[j], weights, f"settle_{j}", [latest], SETTLE)
         if k == parts - 1 and k > 1:
             weights = [[np.eye(len(block)), arrival_weight(block, parts, b, k)] for b in range(parts)]
-            done[j] = mix([done[j], brought[j][-1]], weights, f"finish_{j}", deps)
+            done[j] = mix([done[j], brought[j][-1]], weights, f"finish_{j}", deps, FINISH)
             latest = done[j]
         if k == parts - 1 and j == 0:
             src_prev, src_next = call(
@@ -518,7 +520,7 @@
     planes = pltpu.VMEM((steps + 2, rows + 8, total), jnp.float32)
     return tuple(
         call(
-            functools.partial(final_kernel, parts=places, width=unit),
+            functools.partial(final_kernel, parts=places, width=span),
             done[1:] + [done[0], s_after, s_before, src, src_after, src_before, e, n],
             [f32(steps, rows, total)] * 3,
             "final",

time: 67.4 us -> 66.6 us (0.988)
  no operation moved by 1% of the time
where the time goes in v3:
time: 66.6 us; the launch traced here: 66.2 us
  starting transfers between devices  32.4 us (49%)
  waiting for transfers between devices  20.2 us (30%)
  Pallas kernels  10 us (15%)
  local copies, waits for them, and re-layouts  2.46 us (4%)
  between operations  1.12 us (2%)
    ppermute x15, starting transfers between devices, hop(): return lax.ppermute(x, 'tm', [(k - 1, k), (parts - k, parts - 1 - k)])  26.2 us
    ppermute x15, waiting for transfers between devices, hop(): return lax.ppermute(x, 'tm', [(k - 1, k), (parts - k, parts - 1 - k)])  20.2 us
    pallas_call x25, Pallas kernels, call(): pl.pallas_call(run, out_shape=outs, in_specs=(in_specs or [VMEM] * count)...  10 us
    ppermute x1, starting transfers between devices, body(): after = lax.ppermute(first_rows, 'space', backward)  2.95 us
    ppermute x1, starting transfers between devices, body(): s_after = lax.ppermute(to_prev, 'space', backward)  2.62 us
    unnamed x10, local copies, waits for them, and re-layouts  2.46 us
  transfers between devices with their start and end apart: 21, of which 6 were waited for; matrix products, arithmetic and copies ran while one was open for 0% of the time, Pallas kernels for 6%

profile of v3, /device:TPU:0, one launch (start us, length us, event | category | flops | bytes accessed | tf_op | source)
XLA Modules:
  0.0 66.2 jit_solution(9145304514088703963)
XLA Ops:
  0.6 1.2 %copy-done.1 = f32[8,16,2048]{2,1,0:T(8,128)S(1)} copy-done((f32[8,16,2048]{2,1,0:T(8,128)S(1)}, f32[8,16,2048]{2,1,0:T(8,128)}, u32[]{:S(2)}) %copy-start.1) | copy-done | bytes 1048600
  1.9 1.2 %copy-done.3 = f32[8,16,2048]{2,1,0:T(8,128)S(1)} copy-done((f32[8,16,2048]{2,1,0:T(8,128)S(1)}, f32[8,16,2048]{2,1,0:T(8,128)}, u32[]{:S(2)}) %copy-start.3) | copy-done | bytes 1048600
  3.1 0.6 turn.1
  3.7 0.5 collective-permute-start
  4.2 2.9 %collective-permute-start.1 = (f32[16,2048]{1,0:T(8,128)S(1)}, f32[16,2048]{1,0:T(8,128)S(1)}, u32[]{:S(2)}, u32[]{:S(2)}) collective-permute-start(f32[16,2048]{1,0:T(8,128)S(1)} %get-tuple-element.18), channel_id=1, source_target_pairs={{1,0},{2,1},{3,2},{4,3},{5,4},{6,5},{7,6},{0,7},{9,8},{10,9},{11,1... | collective-permute-start | bytes 393224 | tf_op jit(solution)/shard_map/ppermute | solution.py:467
  7.2 4.2 %collective-permute-start.3 = (f32[2,16,2048]{2,1,0:T(8,128)S(1)}, f32[2,16,2048]{2,1,0:T(8,128)S(1)}, u32[]{:S(2)}, u32[]{:S(2)}) collective-permute-start(f32[2,16,2048]{2,1,0:T(8,128)S(1)} %get-tuple-element.20.refs_1_.refs_0_), channel_id=1, source_target_pairs={{0,8},{24,16},{1,9},{25,17},{2,10},{26,18},{3,11},{27,19},{4,12},{... | collective-permute-start | bytes 786440 | tf_op jit(solution)/shard_map/ppermute | solution.py:454
  11.4 2.3 %source.1 = (f32[8,16,2048]{2,1,0:T(8,128)S(1)}, f32[3,8,2048]{2,1,0:T(8,128)S(1)}, f32[3,8,2048]{2,1,0:T(8,128)S(1)}, f32[7,8,1024]{2,1,0:T(8,128)S(1)}, f32[7,...) custom-call(f32[8,16,2048]{2,1,0:T(8,128)S(1)} %copy-done, ...), custom_call_target="tpu_custom_call" | custom-call | flops 2500000000 | bytes 1000 | tf_op jit(solution)/shard_map/source/pallas_call | solution.py:417
  13.7 2.6 %collective-permute-start.2 = (f32[7,8,1024]{2,1,0:T(8,128)S(1)}, f32[7,8,1024]{2,1,0:T(8,128)S(1)}, u32[]{:S(2)}, u32[]{:S(2)}) collective-permute-start(f32[7,8,1024]{2,1,0:T(8,128)S(1)} %get-tuple-element.19.refs_2_.refs_1_.refs_0_), channel_id=1, source_target_pairs={{0,8},{24,16},{1,9},{25,17},{2,10},{26,18},{3,11},{27,19},{4,12},{... | collective-permute-start | bytes 688136 | tf_op jit(solution)/shard_map/ppermute | solution.py:454
  16.4 0.7 %collective-permute-start.6 = (f32[2,16,2048]{2,1,0:T(8,128)S(1)}, f32[2,16,2048]{2,1,0:T(8,128)S(1)}, u32[]{:S(2)}, u32[]{:S(2)}) collective-permute-start(f32[2,16,2048]{2,1,0:T(8,128)S(1)} %message_0_1.1.refs_2_), channel_id=1, source_target_pairs={{8,16},{16,8},{9,17},{17,9},{10,18},{18,10},{11,19},{19,11},{12,20... | collective-permute-start | bytes 786440 | tf_op jit(solution)/shard_map/ppermute | solution.py:454
  17.1 6.9 %collective-permute-start.5 = (f32[7,8,1024]{2,1,0:T(8,128)S(1)}, f32[7,8,1024]{2,1,0:T(8,128)S(1)}, u32[]{:S(2)}, u32[]{:S(2)}) collective-permute-start(f32[7,8,1024]{2,1,0:T(8,128)S(1)} %get-tuple-element.21.refs_1_.refs_0_), channel_id=1, source_target_pairs={{0,8},{24,16},{1,9},{25,17},{2,10},{26,18},{3,11},{27,19},{4,12},{... | collective-permute-start | bytes 688136 | tf_op jit(solution)/shard_map/ppermute | solution.py:454
  24.0 1.3 %collective-permute-start.9 = (f32[7,8,1024]{2,1,0:T(8,128)S(1)}, f32[7,8,1024]{2,1,0:T(8,128)S(1)}, u32[]{:S(2)}, u32[]{:S(2)}) collective-permute-start(f32[7,8,1024]{2,1,0:T(8,128)S(1)} %get-tuple-element.22.refs_1_.refs_0_), channel_id=1, source_target_pairs={{0,8},{24,16},{1,9},{25,17},{2,10},{26,18},{3,11},{27,19},{4,12},{... | collective-permute-start | bytes 688136 | tf_op jit(solution)/shard_map/ppermute | solution.py:454
  25.3 1.3 %collective-permute-start.13 = (f32[7,8,1024]{2,1,0:T(8,128)S(1)}, f32[7,8,1024]{2,1,0:T(8,128)S(1)}, u32[]{:S(2)}, u32[]{:S(2)}) collective-permute-start(f32[7,8,1024]{2,1,0:T(8,128)S(1)} %get-tuple-element.26.refs_1_.refs_0_), channel_id=1, source_target_pairs={{0,8},{24,16},{1,9},{25,17},{2,10},{26,18},{3,11},{27,19},{4,12},{... | collective-permute-start | bytes 688136 | tf_op jit(solution)/shard_map/ppermute | solution.py:454
  26.7 0.7 %collective-permute-start.4 = (f32[7,8,1024]{2,1,0:T(8,128)S(1)}, f32[7,8,1024]{2,1,0:T(8,128)S(1)}, u32[]{:S(2)}, u32[]{:S(2)}) collective-permute-start(f32[7,8,1024]{2,1,0:T(8,128)S(1)} %message_1_1.1.refs_2_), channel_id=1, source_target_pairs={{8,16},{16,8},{9,17},{17,9},{10,18},{18,10},{11,19},{19,11},{12,20... | collective-permute-start | bytes 688136 | tf_op jit(solution)/shard_map/ppermute | solution.py:454
  27.4 1.3 %collective-permute-start.10 = (f32[2,16,2048]{2,1,0:T(8,128)S(1)}, f32[2,16,2048]{2,1,0:T(8,128)S(1)}, u32[]{:S(2)}, u32[]{:S(2)}) collective-permute-start(f32[2,16,2048]{2,1,0:T(8,128)S(1)} %message_0_2.1.refs_2_.refs_3_), channel_id=1, source_target_pairs={{16,24},{8,0},{17,25},{9,1},{18,26},{10,2},{19,27},{11,3},{20,28},... | collective-permute-start | bytes 786440 | tf_op jit(solution)/shard_map/ppermute | solution.py:454
  28.7 1.3 %collective-permute-done.5.refs_0_.refs_1_ = f32[7,8,1024]{2,1,0:T(8,128)S(1)} collective-permute-done((f32[7,8,1024]{2,1,0:T(8,128)S(1)}, f32[7,8,1024]{2,1,0:T(8,128)S(1)}, u32[]{:S(2)}, u32[]{:S(2)}) %collective-permute-start.5) | collective-permute-done | bytes 229408 | tf_op jit(solution)/shard_map/ppermute | solution.py:454
  30.0 0.7 %collective-permute-start.8 = (f32[7,8,1024]{2,1,0:T(8,128)S(1)}, f32[7,8,1024]{2,1,0:T(8,128)S(1)}, u32[]{:S(2)}, u32[]{:S(2)}) collective-permute-start(f32[7,8,1024]{2,1,0:T(8,128)S(1)} %message_2_1.1.refs_2_), channel_id=1, source_target_pairs={{8,16},{16,8},{9,17},{17,9},{10,18},{18,10},{11,19},{19,11},{12,20... | collective-permute-start | bytes 688136 | tf_op jit(solution)/shard_map/ppermute | solution.py:454
  30.9 1.3 %collective-permute-start.7 = (f32[7,8,1024]{2,1,0:T(8,128)S(1)}, f32[7,8,1024]{2,1,0:T(8,128)S(1)}, u32[]{:S(2)}, u32[]{:S(2)}) collective-permute-start(f32[7,8,1024]{2,1,0:T(8,128)S(1)} %message_1_2.1.refs_3_.refs_2_), channel_id=1, source_target_pairs={{16,24},{8,0},{17,25},{9,1},{18,26},{10,2},{19,27},{11,3},{20,28},... | collective-permute-start | bytes 688136 | tf_op jit(solution)/shard_map/ppermute | solution.py:454
  32.2 0.1 settle_1.1.refs_0_
  32.3 4.9 %collective-permute-done.10.refs_1_ = f32[2,16,2048]{2,1,0:T(8,128)S(1)} collective-permute-done((f32[2,16,2048]{2,1,0:T(8,128)S(1)}, f32[2,16,2048]{2,1,0:T(8,128)S(1)}, u32[]{:S(2)}, u32[]{:S(2)}) %collective-permute-start.10) | collective-permute-done | bytes 262176 | tf_op jit(solution)/shard_map/ppermute | solution.py:454
  37.5 0.7 %collective-permute-start.12 = (f32[7,8,1024]{2,1,0:T(8,128)S(1)}, f32[7,8,1024]{2,1,0:T(8,128)S(1)}, u32[]{:S(2)}, u32[]{:S(2)}) collective-permute-start(f32[7,8,1024]{2,1,0:T(8,128)S(1)} %message_3_1.1.refs_2_), channel_id=1, source_target_pairs={{8,16},{16,8},{9,17},{17,9},{10,18},{18,10},{11,19},{19,11},{12,20... | collective-permute-start | bytes 688136 | tf_op jit(solution)/shard_map/ppermute | solution.py:454
  38.2 1.3 %collective-permute-start.11 = (f32[7,8,1024]{2,1,0:T(8,128)S(1)}, f32[7,8,1024]{2,1,0:T(8,128)S(1)}, u32[]{:S(2)}, u32[]{:S(2)}) collective-permute-start(f32[7,8,1024]{2,1,0:T(8,128)S(1)} %message_2_2.1.refs_2_.refs_3_), channel_id=1, source_target_pairs={{16,24},{8,0},{17,25},{9,1},{18,26},{10,2},{19,27},{11,3},{20,28},... | collective-permute-start | bytes 688136 | tf_op jit(solution)/shard_map/ppermute | solution.py:454
  39.5 0.1 settle_2.1.refs_0_
  39.6 1.4 %collective-permute-done.7.refs_1_ = f32[7,8,1024]{2,1,0:T(8,128)S(1)} collective-permute-done((f32[7,8,1024]{2,1,0:T(8,128)S(1)}, f32[7,8,1024]{2,1,0:T(8,128)S(1)}, u32[]{:S(2)}, u32[]{:S(2)}) %collective-permute-start.7) | collective-permute-done | bytes 229408 | tf_op jit(solution)/shard_map/ppermute | solution.py:454
  41.2 0.7 %collective-permute-start.15 = (f32[7,8,1024]{2,1,0:T(8,128)S(1)}, f32[7,8,1024]{2,1,0:T(8,128)S(1)}, u32[]{:S(2)}, u32[]{:S(2)}) collective-permute-start(f32[7,8,1024]{2,1,0:T(8,128)S(1)} %message_4_1.1.refs_2_), channel_id=1, source_target_pairs={{8,16},{16,8},{9,17},{17,9},{10,18},{18,10},{11,19},{19,11},{12,20... | collective-permute-start | bytes 688136 | tf_op jit(solution)/shard_map/ppermute | solution.py:454
  41.9 1.3 %collective-permute-start.14 = (f32[7,8,1024]{2,1,0:T(8,128)S(1)}, f32[7,8,1024]{2,1,0:T(8,128)S(1)}, u32[]{:S(2)}, u32[]{:S(2)}) collective-permute-start(f32[7,8,1024]{2,1,0:T(8,128)S(1)} %message_3_2.1.refs_2_.refs_3_), channel_id=1, source_target_pairs={{16,24},{8,0},{17,25},{9,1},{18,26},{10,2},{19,27},{11,3},{20,28},... | collective-permute-start | bytes 688136 | tf_op jit(solution)/shard_map/ppermute | solution.py:454
  43.2 5.1 %collective-permute-done.11.refs_1_ = f32[7,8,1024]{2,1,0:T(8,128)S(1)} collective-permute-done((f32[7,8,1024]{2,1,0:T(8,128)S(1)}, f32[7,8,1024]{2,1,0:T(8,128)S(1)}, u32[]{:S(2)}, u32[]{:S(2)}) %collective-permute-start.11) | collective-permute-done | bytes 229408 | tf_op jit(solution)/shard_map/ppermute | solution.py:454
  48.5 1.3 %collective-permute-start.18 = (f32[7,8,1024]{2,1,0:T(8,128)S(1)}, f32[7,8,1024]{2,1,0:T(8,128)S(1)}, u32[]{:S(2)}, u32[]{:S(2)}) collective-permute-start(f32[7,8,1024]{2,1,0:T(8,128)S(1)} %message_4_2.1.refs_2_.refs_3_), channel_id=1, source_target_pairs={{16,24},{8,0},{17,25},{9,1},{18,26},{10,2},{19,27},{11,3},{20,28},... | collective-permute-start | bytes 688136 | tf_op jit(solution)/shard_map/ppermute | solution.py:454
  49.9 2.6 %collective-permute-start.19 = (f32[3,8,2048]{2,1,0:T(8,128)S(1)}, f32[3,8,2048]{2,1,0:T(8,128)S(1)}, u32[]{:S(2)}, u32[]{:S(2)}) collective-permute-start(f32[3,8,2048]{2,1,0:T(8,128)S(1)} %get-tuple-element.27.refs_2_), channel_id=1, source_target_pairs={{1,0},{2,1},{3,2},{4,3},{5,4},{6,5},{7,6},{0,7},{9,8},{10,9},{11,1... | collective-permute-start | bytes 589832 | tf_op jit(solution)/shard_map/ppermute | solution.py:517
  52.6 0.1 settle_4.1.refs_0_
  52.8 1.2 %collective-permute-done.14.refs_1_ = f32[7,8,1024]{2,1,0:T(8,128)S(1)} collective-permute-done((f32[7,8,1024]{2,1,0:T(8,128)S(1)}, f32[7,8,1024]{2,1,0:T(8,128)S(1)}, u32[]{:S(2)}, u32[]{:S(2)}) %collective-permute-start.14) | collective-permute-done | bytes 229408 | tf_op jit(solution)/shard_map/ppermute | solution.py:454
  54.1 6.3 %collective-permute-done.18.refs_1_ = f32[7,8,1024]{2,1,0:T(8,128)S(1)} collective-permute-done((f32[7,8,1024]{2,1,0:T(8,128)S(1)}, f32[7,8,1024]{2,1,0:T(8,128)S(1)}, u32[]{:S(2)}, u32[]{:S(2)}) %collective-permute-start.18) | collective-permute-done | bytes 229408 | tf_op jit(solution)/shard_map/ppermute | solution.py:454
  60.5 5.6 %final.1 = (f32[8,16,2048]{2,1,0:T(8,128)}, f32[8,16,2048]{2,1,0:T(8,128)}, f32[8,16,2048]{2,1,0:T(8,128)}) custom-call(f32[7,8,1024]{2,1,0:T(8,128)S(1)} %finish_1.1.refs_2_.refs_0_, f32[7,8,1024]{2,1,0:T(8,128)S(1)} %finish_2.1.refs_1_, f32[7,8,1024]{2,1,0:T(8,128)S(1)} %finish_3.1.refs_2_, f32[7,8,1024]{2,1,0:T(8,128)S(1)} %finish_4.1.refs_3_, ...), custom_call_target="tpu_custom_call" | custom-call | flops 2500000000 | bytes 1000 | tf_op jit(solution)/shard_map/final/pallas_call | solution.py:417
  (45 shorter events, 1.3 us)
Async XLA Ops:
  0.6 1.2 %copy-start.1 = (f32[8,16,2048]{2,1,0:T(8,128)S(1)}, f32[8,16,2048]{2,1,0:T(8,128)}, u32[]{:S(2)}) copy-start(f32[8,16,2048]{2,1,0:T(8,128)} %refs_10_.1) | copy-start | bytes 3145732
  1.9 1.2 %copy-start.3 = (f32[8,16,2048]{2,1,0:T(8,128)S(1)}, f32[8,16,2048]{2,1,0:T(8,128)}, u32[]{:S(2)}) copy-start(f32[8,16,2048]{2,1,0:T(8,128)} %refs_11_.1) | copy-start | bytes 3145732
  3.1 8.3 %copy-start = (f32[8,16,2048]{2,1,0:T(8,128)S(1)}, f32[8,16,2048]{2,1,0:T(8,128)}, u32[]{:S(2)}) copy-start(f32[8,16,2048]{2,1,0:T(8,128)} %refs_0_.3) | copy-start | bytes 3145732
  3.7 7.6 %collective-permute-start = (f32[16,2048]{1,0:T(8,128)S(1)}, f32[16,2048]{1,0:T(8,128)S(1)}, u32[]{:S(2)}, u32[]{:S(2)}) collective-permute-start(f32[16,2048]{1,0:T(8,128)S(1)} %get-tuple-element.17), channel_id=1, source_target_pairs={{0,1},{1,2},{2,3},{3,4},{4,5},{5,6},{6,7},{7,0},{8,9},{9,10},{10,1... | collective-permute-start | bytes 393224 | tf_op jit(solution)/shard_map/ppermute | solution.py:466
  4.2 7.1 %collective-permute-start.1 = (f32[16,2048]{1,0:T(8,128)S(1)}, f32[16,2048]{1,0:T(8,128)S(1)}, u32[]{:S(2)}, u32[]{:S(2)}) collective-permute-start(f32[16,2048]{1,0:T(8,128)S(1)} %get-tuple-element.18), channel_id=1, source_target_pairs={{1,0},{2,1},{3,2},{4,3},{5,4},{6,5},{7,6},{0,7},{9,8},{10,9},{11,1... | collective-permute-start | bytes 393224 | tf_op jit(solution)/shard_map/ppermute | solution.py:467
  7.2 9.2 %collective-permute-start.3 = (f32[2,16,2048]{2,1,0:T(8,128)S(1)}, f32[2,16,2048]{2,1,0:T(8,128)S(1)}, u32[]{:S(2)}, u32[]{:S(2)}) collective-permute-start(f32[2,16,2048]{2,1,0:T(8,128)S(1)} %get-tuple-element.20.refs_1_.refs_0_), channel_id=1, source_target_pairs={{0,8},{24,16},{1,9},{25,17},{2,10},{26,18},{3,11},{27,19},{4,12},{... | collective-permute-start | bytes 786440 | tf_op jit(solution)/shard_map/ppermute | solution.py:454
  13.7 12.9 %collective-permute-start.2 = (f32[7,8,1024]{2,1,0:T(8,128)S(1)}, f32[7,8,1024]{2,1,0:T(8,128)S(1)}, u32[]{:S(2)}, u32[]{:S(2)}) collective-permute-start(f32[7,8,1024]{2,1,0:T(8,128)S(1)} %get-tuple-element.19.refs_2_.refs_1_.refs_0_), channel_id=1, source_target_pairs={{0,8},{24,16},{1,9},{25,17},{2,10},{26,18},{3,11},{27,19},{4,12},{... | collective-permute-start | bytes 688136 | tf_op jit(solution)/shard_map/ppermute | solution.py:454
  16.4 11.0 %collective-permute-start.6 = (f32[2,16,2048]{2,1,0:T(8,128)S(1)}, f32[2,16,2048]{2,1,0:T(8,128)S(1)}, u32[]{:S(2)}, u32[]{:S(2)}) collective-permute-start(f32[2,16,2048]{2,1,0:T(8,128)S(1)} %message_0_1.1.refs_2_), channel_id=1, source_target_pairs={{8,16},{16,8},{9,17},{17,9},{10,18},{18,10},{11,19},{19,11},{12,20... | collective-permute-start | bytes 786440 | tf_op jit(solution)/shard_map/ppermute | solution.py:454
  17.1 13.0 %collective-permute-start.5 = (f32[7,8,1024]{2,1,0:T(8,128)S(1)}, f32[7,8,1024]{2,1,0:T(8,128)S(1)}, u32[]{:S(2)}, u32[]{:S(2)}) collective-permute-start(f32[7,8,1024]{2,1,0:T(8,128)S(1)} %get-tuple-element.21.refs_1_.refs_0_), channel_id=1, source_target_pairs={{0,8},{24,16},{1,9},{25,17},{2,10},{26,18},{3,11},{27,19},{4,12},{... | collective-permute-start | bytes 688136 | tf_op jit(solution)/shard_map/ppermute | solution.py:454
  24.0 13.4 %collective-permute-start.9 = (f32[7,8,1024]{2,1,0:T(8,128)S(1)}, f32[7,8,1024]{2,1,0:T(8,128)S(1)}, u32[]{:S(2)}, u32[]{:S(2)}) collective-permute-start(f32[7,8,1024]{2,1,0:T(8,128)S(1)} %get-tuple-element.22.refs_1_.refs_0_), channel_id=1, source_target_pairs={{0,8},{24,16},{1,9},{25,17},{2,10},{26,18},{3,11},{27,19},{4,12},{... | collective-permute-start | bytes 688136 | tf_op jit(solution)/shard_map/ppermute | solution.py:454
  25.3 15.8 %collective-permute-start.13 = (f32[7,8,1024]{2,1,0:T(8,128)S(1)}, f32[7,8,1024]{2,1,0:T(8,128)S(1)}, u32[]{:S(2)}, u32[]{:S(2)}) collective-permute-start(f32[7,8,1024]{2,1,0:T(8,128)S(1)} %get-tuple-element.26.refs_1_.refs_0_), channel_id=1, source_target_pairs={{0,8},{24,16},{1,9},{25,17},{2,10},{26,18},{3,11},{27,19},{4,12},{... | collective-permute-start | bytes 688136 | tf_op jit(solution)/shard_map/ppermute | solution.py:454
  26.7 4.2 %collective-permute-start.4 = (f32[7,8,1024]{2,1,0:T(8,128)S(1)}, f32[7,8,1024]{2,1,0:T(8,128)S(1)}, u32[]{:S(2)}, u32[]{:S(2)}) collective-permute-start(f32[7,8,1024]{2,1,0:T(8,128)S(1)} %message_1_1.1.refs_2_), channel_id=1, source_target_pairs={{8,16},{16,8},{9,17},{17,9},{10,18},{18,10},{11,19},{19,11},{12,20... | collective-permute-start | bytes 688136 | tf_op jit(solution)/shard_map/ppermute | solution.py:454
  27.4 9.8 %collective-permute-start.10 = (f32[2,16,2048]{2,1,0:T(8,128)S(1)}, f32[2,16,2048]{2,1,0:T(8,128)S(1)}, u32[]{:S(2)}, u32[]{:S(2)}) collective-permute-start(f32[2,16,2048]{2,1,0:T(8,128)S(1)} %message_0_2.1.refs_2_.refs_3_), channel_id=1, source_target_pairs={{16,24},{8,0},{17,25},{9,1},{18,26},{10,2},{19,27},{11,3},{20,28},... | collective-permute-start | bytes 786440 | tf_op jit(solution)/shard_map/ppermute | solution.py:454
  30.0 8.1 %collective-permute-start.8 = (f32[7,8,1024]{2,1,0:T(8,128)S(1)}, f32[7,8,1024]{2,1,0:T(8,128)S(1)}, u32[]{:S(2)}, u32[]{:S(2)}) collective-permute-start(f32[7,8,1024]{2,1,0:T(8,128)S(1)} %message_2_1.1.refs_2_), channel_id=1, source_target_pairs={{8,16},{16,8},{9,17},{17,9},{10,18},{18,10},{11,19},{19,11},{12,20... | collective-permute-start | bytes 688136 | tf_op jit(solution)/shard_map/ppermute | solution.py:454
  30.9 10.1 %collective-permute-start.7 = (f32[7,8,1024]{2,1,0:T(8,128)S(1)}, f32[7,8,1024]{2,1,0:T(8,128)S(1)}, u32[]{:S(2)}, u32[]{:S(2)}) collective-permute-start(f32[7,8,1024]{2,1,0:T(8,128)S(1)} %message_1_2.1.refs_3_.refs_2_), channel_id=1, source_target_pairs={{16,24},{8,0},{17,25},{9,1},{18,26},{10,2},{19,27},{11,3},{20,28},... | collective-permute-start | bytes 688136 | tf_op jit(solution)/shard_map/ppermute | solution.py:454
  37.4 15.4 %collective-permute-start.16 = (f32[4,8,2048]{2,1,0:T(8,128)S(1)}, f32[4,8,2048]{2,1,0:T(8,128)S(1)}, u32[]{:S(2)}, u32[]{:S(2)}) collective-permute-start(f32[4,8,2048]{2,1,0:T(8,128)S(1)} %get-tuple-element.25.refs_2_), channel_id=1, source_target_pairs={{1,0},{2,1},{3,2},{4,3},{5,4},{6,5},{7,6},{0,7},{9,8},{10,9},{11,1... | collective-permute-start | bytes 786440 | tf_op jit(solution)/shard_map/ppermute | solution.py:507
  37.5 4.4 %collective-permute-start.12 = (f32[7,8,1024]{2,1,0:T(8,128)S(1)}, f32[7,8,1024]{2,1,0:T(8,128)S(1)}, u32[]{:S(2)}, u32[]{:S(2)}) collective-permute-start(f32[7,8,1024]{2,1,0:T(8,128)S(1)} %message_3_1.1.refs_2_), channel_id=1, source_target_pairs={{8,16},{16,8},{9,17},{17,9},{10,18},{18,10},{11,19},{19,11},{12,20... | collective-permute-start | bytes 688136 | tf_op jit(solution)/shard_map/ppermute | solution.py:454
  38.2 10.1 %collective-permute-start.11 = (f32[7,8,1024]{2,1,0:T(8,128)S(1)}, f32[7,8,1024]{2,1,0:T(8,128)S(1)}, u32[]{:S(2)}, u32[]{:S(2)}) collective-permute-start(f32[7,8,1024]{2,1,0:T(8,128)S(1)} %message_2_2.1.refs_2_.refs_3_), channel_id=1, source_target_pairs={{16,24},{8,0},{17,25},{9,1},{18,26},{10,2},{19,27},{11,3},{20,28},... | collective-permute-start | bytes 688136 | tf_op jit(solution)/shard_map/ppermute | solution.py:454
  41.0 8.9 %collective-permute-start.17 = (f32[4,8,2048]{2,1,0:T(8,128)S(1)}, f32[4,8,2048]{2,1,0:T(8,128)S(1)}, u32[]{:S(2)}, u32[]{:S(2)}) collective-permute-start(f32[4,8,2048]{2,1,0:T(8,128)S(1)} %get-tuple-element.28), channel_id=1, source_target_pairs={{0,1},{1,2},{2,3},{3,4},{4,5},{5,6},{6,7},{7,0},{8,9},{9,10},{10,1... | collective-permute-start | bytes 786440 | tf_op jit(solution)/shard_map/ppermute | solution.py:508
  41.2 7.3 %collective-permute-start.15 = (f32[7,8,1024]{2,1,0:T(8,128)S(1)}, f32[7,8,1024]{2,1,0:T(8,128)S(1)}, u32[]{:S(2)}, u32[]{:S(2)}) collective-permute-start(f32[7,8,1024]{2,1,0:T(8,128)S(1)} %message_4_1.1.refs_2_), channel_id=1, source_target_pairs={{8,16},{16,8},{9,17},{17,9},{10,18},{18,10},{11,19},{19,11},{12,20... | collective-permute-start | bytes 688136 | tf_op jit(solution)/shard_map/ppermute | solution.py:454
  41.9 12.1 %collective-permute-start.14 = (f32[7,8,1024]{2,1,0:T(8,128)S(1)}, f32[7,8,1024]{2,1,0:T(8,128)S(1)}, u32[]{:S(2)}, u32[]{:S(2)}) collective-permute-start(f32[7,8,1024]{2,1,0:T(8,128)S(1)} %message_3_2.1.refs_2_.refs_3_), channel_id=1, source_target_pairs={{16,24},{8,0},{17,25},{9,1},{18,26},{10,2},{19,27},{11,3},{20,28},... | collective-permute-start | bytes 688136 | tf_op jit(solution)/shard_map/ppermute | solution.py:454
  48.5 11.9 %collective-permute-start.18 = (f32[7,8,1024]{2,1,0:T(8,128)S(1)}, f32[7,8,1024]{2,1,0:T(8,128)S(1)}, u32[]{:S(2)}, u32[]{:S(2)}) collective-permute-start(f32[7,8,1024]{2,1,0:T(8,128)S(1)} %message_4_2.1.refs_2_.refs_3_), channel_id=1, source_target_pairs={{16,24},{8,0},{17,25},{9,1},{18,26},{10,2},{19,27},{11,3},{20,28},... | collective-permute-start | bytes 688136 | tf_op jit(solution)/shard_map/ppermute | solution.py:454
  49.8 10.7 %collective-permute-start.20 = (f32[3,8,2048]{2,1,0:T(8,128)S(1)}, f32[3,8,2048]{2,1,0:T(8,128)S(1)}, u32[]{:S(2)}, u32[]{:S(2)}) collective-permute-start(f32[3,8,2048]{2,1,0:T(8,128)S(1)} %get-tuple-element.29), channel_id=1, source_target_pairs={{0,1},{1,2},{2,3},{3,4},{4,5},{5,6},{6,7},{7,0},{8,9},{9,10},{10,1... | collective-permute-start | bytes 589832 | tf_op jit(solution)/shard_map/ppermute | solution.py:518
  49.9 10.6 %collective-permute-start.19 = (f32[3,8,2048]{2,1,0:T(8,128)S(1)}, f32[3,8,2048]{2,1,0:T(8,128)S(1)}, u32[]{:S(2)}, u32[]{:S(2)}) collective-permute-start(f32[3,8,2048]{2,1,0:T(8,128)S(1)} %get-tuple-element.27.refs_2_), channel_id=1, source_target_pairs={{1,0},{2,1},{3,2},{4,3},{5,4},{6,5},{7,6},{0,7},{9,8},{10,9},{11,1... | collective-permute-start | bytes 589832 | tf_op jit(solution)/shard_map/ppermute | solution.py:517
  52.8 7.8 %copy-start.2 = (f32[8,16,2048]{2,1,0:T(8,128)S(1)}, f32[8,16,2048]{2,1,0:T(8,128)}, u32[]{:S(2)}) copy-start(f32[8,16,2048]{2,1,0:T(8,128)} %refs_10_.1) | copy-start | bytes 3145732
  52.8 7.8 %copy-start.4 = (f32[8,16,2048]{2,1,0:T(8,128)S(1)}, f32[8,16,2048]{2,1,0:T(8,128)}, u32[]{:S(2)}) copy-start(f32[8,16,2048]{2,1,0:T(8,128)} %refs_11_.1) | copy-start | bytes 3145732
